TPU v7x, 32 devices: a whole 2x2x4 slice. The times are simulated.
32 devices in a mesh: wide: 8 (over y, x, core), narrow: 4 (over z).
Axes of the slice: x: 2, y: 2, z: 4, core: 2. Of those that a mesh axis runs over, the one named last changes fastest.
Arguments:
- points: float32 [8, 16384], P(None, 'narrow'), may hold values from 0 to 1
- scales: float32 [8], replicated, may hold values from 2 to 6
- frequencies: float32 [8, 32768], P(None, 'wide'), may hold values from -24 to 24
- phases: float32 [32768], P('wide'), may hold values from -3.140625 to 3.140625
- feature_weights: bfloat16 [64, 32768], P(None, 'wide'), may hold values from -6 to 6
- targets: float32 [16384], P(('narrow', 'wide')), may hold values from -6 to 6
- noise: float32 [64, 16384], P(None, ('narrow', 'wide')), may hold values from -1.8 to 1.8
- inverses: float32 [2, 8192, 8192], P(None, 'wide', 'narrow'), may hold values from -0.01767767 to 1.0176777
- groups: int32 [2, 64], replicated, may hold values from 0 to 127, as said below
Outputs:
- residual: float32 [64, 16384], P(None, ('narrow', 'wide'))
- weights: float32 [2, 64, 8192], P(None, None, 'wide')
Inputs may be any that keep to these rules, and one draw needn't show every extreme that they name: All entries differ; each names the group of points g * 128 to g * 128 + 127. In every block, the entries n * 16 to (n + 1) * 16 - 1 name groups of narrow index n's points, that is groups n * 32 to (n + 1) * 32 - 1.
All inputs are finite; a program needn't handle non-finite values.
Results may differ from a plain program's by a relative error of at most 0.00065.
Values may be sent and summed in bfloat16 or wider, within the bound.
No kernel may reach another device: no remote copies, remote signals or barrier semaphores. Data moves between devices by JAX's collectives and lax.ppermute only.
A program may use at most 128 MiB of HBM per device.

v0:
```python
import functools
import math
from typing import NamedTuple

import jax
import jax.numpy as jnp
from jax import lax
from jax.experimental import pallas as pl
from jax.experimental.pallas import tpu as pltpu
from jax.sharding import PartitionSpec as P

GROUP = 128
BLOCKS = 2
NOISE_VAR = 0.1
LN2 = math.log(2.0)
TO_TURNS = 1.0 / (2.0 * math.pi)
TO_U = math.sqrt(5.0) / LN2
SINE = (-6.283164044164058, 41.33714235333657, -81.34076831835199, 70.99342806157215)
FIRST = 58
F32 = jnp.float32
BF16 = jnp.bfloat16


class Sizes(NamedTuple):
    shard: int
    share: int
    own: int
    rows: int


def thirds(x):
    high = x.astype(BF16).astype(F32)
    rest = x - high
    mid = rest.astype(BF16).astype(F32)
    low = (rest - mid).astype(BF16).astype(F32)
    return high, mid, low


def halves(x):
    high = x.astype(BF16)
    return high, (x - high.astype(F32)).astype(BF16)


def stack_rows(rows):
    width = max(row.shape[1] for row in rows)
    at = lax.broadcasted_iota(jnp.int32, (8, width), 0)
    out = jnp.zeros((8, width), F32)
    for index, row in enumerate(rows):
        out = jnp.where(at == index, row, out)
    return out


def left_terms(parts, extra):
    high, mid, low = parts
    return jnp.concatenate([high, high, mid, mid, high, low, extra, jnp.zeros_like(high)], 0)


def right_terms(parts, extra):
    high, mid, low = parts
    return jnp.concatenate([high, mid, high, mid, low, high, extra, jnp.zeros_like(high)], 0)


def cosine(turns):
    fraction = turns - jnp.round(turns)
    shifted = jnp.abs(fraction) - 0.25
    square = shifted * shifted
    value = SINE[-1]
    for factor in SINE[-2::-1]:
        value = value * square + factor
    return value * shifted


def group_cut(inside):
    return pl.ds(pl.multiple_of(inside * GROUP, GROUP), GROUP)


def group_of(ref, index):
    return ref[:, pl.ds(pl.multiple_of(index * GROUP, GROUP), GROUP)]


def dots(terms, high, low, samples):
    both = jnp.dot(terms, high, preferred_element_type=F32)
    return both[:samples] + both[samples:] + jnp.dot(terms[:samples], low, preferred_element_type=F32)


def two_parts(x):
    high, low = halves(x)
    return jnp.concatenate([high, low], 0)


def core_of(side):
    core = lax.rem(lax.axis_index("wide"), 2)
    return core if side else 1 - core


class Block(NamedTuple):
    block: int
    side: int
    begin: int
    count: int

    def at(self, sizes, table, k):
        narrow = lax.axis_index("narrow")
        entry = narrow * sizes.share + core_of(self.side) * (sizes.share // 2) + self.begin + k
        return table[self.block, entry] - narrow * sizes.shard


class Other(NamedTuple):
    begin: int
    count: int

    def at(self, sizes, table, k):
        return table[self.begin + k]


class Natural(NamedTuple):
    side: int
    begin: int
    count: int

    def at(self, sizes, table, k):
        part = self.begin + k // sizes.own
        return (2 * part + core_of(self.side)) * sizes.own + k % sizes.own


def row_group(sizes, table, block, j):
    group = table[block, lax.axis_index("wide") * sizes.rows + j]
    return group // sizes.shard, lax.rem(group, sizes.shard)


def call(body, name, shapes, tables, arrays, flops, after=(), scratch=(), kinds=None, limit=6):
    kinds = kinds or [pltpu.VMEM] * len(arrays)
    spaces = [pltpu.SMEM] * len(tables) + kinds + [pl.ANY] * len(after)

    def run(*refs):
        inputs = len(tables) + len(arrays)
        body(*refs[:inputs], *refs[inputs + len(after) :])

    return pl.pallas_call(
        run,
        out_shape=[jax.ShapeDtypeStruct(*shape) for shape in shapes],
        in_specs=[pl.BlockSpec(memory_space=space) for space in spaces],
        out_specs=[pl.BlockSpec(memory_space=pltpu.VMEM)] * len(shapes),
        scratch_shapes=list(scratch),
        compiler_params=pltpu.CompilerParams(vmem_limit_bytes=limit << 20),
        cost_estimate=pl.CostEstimate(flops=int(flops), bytes_accessed=0, transcendentals=0),
        name=name,
    )(*tables, *arrays, *after)


def loop(count, body, start=None):
    if count == 1:
        return body(0, start)
    return lax.fori_loop(0, count, body, start)


def prior_tiles(sizes, which, factor, table, left, fw, points, targets, noise, out):
    features, width = left.shape[0], out.shape[1]
    tile, chunk = math.gcd(width, 512), math.gcd(features, 2048)
    per = tile // GROUP
    ones = jnp.ones((1, tile), F32)

    def one_tile(at, _):
        groups = [which.at(sizes, table, at * per + k) for k in range(per)]
        coords = jnp.concatenate([group_of(points, group) for group in groups], 1)
        right = right_terms(thirds(coords), stack_rows([ones] * 3)).astype(BF16)

        def one_chunk(index, total):
            cut = pl.ds(pl.multiple_of(index * chunk, chunk), chunk)
            turns = jnp.dot(left[cut, :], right, preferred_element_type=F32)
            values = cosine(turns).astype(BF16)
            return total + jnp.dot(fw[:, cut], values, preferred_element_type=F32)

        total = loop(features // chunk, one_chunk, jnp.zeros((out.shape[0], tile), F32))
        out[:, pl.ds(pl.multiple_of(at * tile, tile), tile)] = -factor * total
        for k, group in enumerate(groups):

            @pl.when(group // sizes.own == lax.axis_index("wide"))
            def _():
                inside = lax.rem(group, sizes.own)
                out[:, group_cut(at * per + k)] += group_of(targets, inside) - group_of(noise, inside)

        return 0

    loop(width // tile, one_tile, 0)


def first_body(sizes, which, factor, table, *refs):
    sources, (out, left, picked), held, sems = refs[:6], refs[6:9], refs[9:15], refs[15]
    copies = [
        pltpu.make_async_copy(source, target, sems.at[index])
        for index, (source, target) in enumerate(zip(sources, held))
    ]
    for copy in copies:
        copy.start()
    freq, phase, points, fw, targets, noise = held
    copies[0].wait()
    copies[1].wait()
    features = freq.shape[1]
    step = math.gcd(features, 1024)

    def one_step(index, _):
        cut = pl.ds(pl.multiple_of(index * step, step), step)
        extra = stack_rows(thirds(phase[:, cut] * TO_TURNS))
        terms = left_terms(thirds(freq[:, cut] * TO_TURNS), extra)
        left[cut, :] = terms.T.astype(BF16)
        return 0

    loop(features // step, one_step, 0)
    copies[2].wait()
    for block in range(BLOCKS):
        for j in range(sizes.rows):
            owner, inside = row_group(sizes, table, block, j)
            mine = jnp.where(owner == lax.axis_index("narrow"), 1.0, 0.0)
            picked[block, :, j * GROUP : (j + 1) * GROUP] = group_of(points, inside) * mine
    for copy in copies[3:]:
        copy.wait()
    prior_tiles(sizes, which, factor, table, left, fw, points, targets, noise, out)


def prior_first(sizes, which, factor, table, arrays):
    freq, fw = arrays[0], arrays[3]
    samples, features = fw.shape
    width = which.count * GROUP
    shapes = [
        ((samples, width), F32),
        ((features, 64), BF16),
        ((BLOCKS, freq.shape[0], sizes.rows * GROUP), F32),
    ]
    scratch = [pltpu.VMEM(array.shape, array.dtype) for array in arrays]
    return call(
        functools.partial(first_body, sizes, which, factor),
        "prior_first",
        shapes,
        (table,),
        arrays,
        2300 * features * width,
        scratch=[*scratch, pltpu.SemaphoreType.DMA((len(arrays),))],
        kinds=[pltpu.HBM] * len(arrays),
        limit=FIRST,
    )


def prior_part(sizes, which, factor, table, arrays, name, after=(), cost=800):
    (samples, features), width = arrays[1].shape, which.count * GROUP
    return call(
        functools.partial(prior_tiles, sizes, which, factor),
        name,
        [((samples, width), F32)],
        (table,),
        arrays,
        cost * features * width,
        after,
        limit=14,
    )[0]


def inverse_body(block, side, x, inverses, *refs):
    *before, out = refs
    samples, depth = x.shape
    rows = out.shape[1]
    tile = math.gcd(rows, 512)
    span = pl.ds(pl.multiple_of(core_of(side) * depth, depth), depth)
    high, low = halves(x[...])
    turned = jnp.concatenate([high.astype(F32), low.astype(F32)], 0).T.astype(BF16)
    for row in range(0, rows, tile):
        cut = slice(row, row + tile)
        high, low = halves(inverses[block, cut, span])
        total = jnp.dot(high, turned, preferred_element_type=F32)
        total += jnp.dot(low, turned, preferred_element_type=F32)
        total = total.T
        total = total[:samples] + total[samples:]
        out[:, cut] = total + before[0][:, cut] if before else total


def inverse_part(x, inverses, block, side, before, name):
    rows, depth = inverses.shape[1], x.shape[1]
    return call(
        functools.partial(inverse_body, block, side),
        name,
        [((x.shape[0], rows), F32)],
        (),
        (x, inverses, *before),
        512 * depth * rows,
    )[0]


def add_body(count, *refs):
    terms, outs = refs[: 2 * count], refs[2 * count :]
    rows = [terms[k][...] + terms[count + k][...] for k in range(count)]
    if len(rows) == len(outs):
        for out, row in zip(outs, rows):
            out[...] = row
    elif len(rows) == 1:
        middle = rows[0].shape[0] // 2
        outs[0][...] = rows[0][:middle]
        outs[1][...] = rows[0][middle:]
    else:
        middle = rows[0].shape[0]
        outs[0][:middle] = rows[0]
        outs[0][middle:] = rows[1]


def add(left, right, outs, after, name):
    rows = sum(array.shape[0] for array in left) // outs
    shapes = [((rows, left[0].shape[1]), F32)] * outs
    return call(
        functools.partial(add_body, len(left)), name, shapes, (), (*left, *right), 1e8, after
    )


def kernel_coords(coords, scales):
    centred = (coords - 0.5) * (scales * TO_U)
    return centred, jnp.sum(centred * centred, axis=0, keepdims=True)


def lefts_body(rows, scales, out):
    for block in range(rows.shape[0]):
        for begin in range(0, rows.shape[2], GROUP):
            cut = slice(begin, begin + GROUP)
            centred, norm = kernel_coords(rows[block, :, cut], scales[...])
            ones = jnp.ones((1, GROUP), F32)
            extra = stack_rows([*thirds(norm), ones, ones, ones])
            matrix = left_terms([-2.0 * part for part in thirds(centred)], extra)
            out[block, cut, :] = matrix.T.astype(BF16)


def lefts_part(rows, scales, after):
    shape = (rows.shape[0], rows.shape[2], 64)
    return call(lefts_body, "lefts", [(shape, BF16)], (), (rows, scales), 1e8, after)[0]


def tiles_of(left, right):
    square = jnp.maximum(jnp.dot(left, right, preferred_element_type=F32), 1e-20)
    u = square * lax.rsqrt(square)
    values = (1.0 + u * (LN2 + (LN2 * LN2 / 3.0) * u)) * jnp.exp2(-u)
    return halves(values)


def right_of(sizes, which, table, points, scales, at, per):
    groups = [which.at(sizes, table, at * per + k) for k in range(per)]
    coords = jnp.concatenate([group_of(points, group) for group in groups], 1)
    centred, norm = kernel_coords(coords, scales[...])
    ones = jnp.ones((1, per * GROUP), F32)
    extra = stack_rows([ones, ones, ones, *thirds(norm)])
    return right_terms(thirds(centred), extra).astype(BF16)


def tiles_body(sizes, which, block, table, lefts, points, scales, high_out, low_out):
    depth, width = high_out.shape
    tile = math.gcd(width, 512)

    def one_tile(at, _):
        right = right_of(sizes, which, table, points, scales, at, tile // GROUP)
        here = pl.ds(pl.multiple_of(at * tile, tile), tile)
        high_out[:, here], low_out[:, here] = tiles_of(lefts[block], right)
        return 0

    loop(width // tile, one_tile, 0)


def tiles_part(sizes, which, block, table, lefts, points, scales, name, after=()):
    depth, width = lefts.shape[1], which.count * GROUP
    return call(
        functools.partial(tiles_body, sizes, which, block),
        name,
        [((depth, width), BF16)] * 2,
        (table,),
        (lefts, points, scales),
        300 * depth * width,
        after,
        limit=10,
    )


def product_body(update, high, low, carry, out):
    samples, width = carry.shape
    terms = two_parts(update[...])
    tile = math.gcd(width, 256)
    for begin in range(0, width, tile):
        cut = slice(begin, begin + tile)
        out[:, cut] = carry[:, cut] - dots(terms, high[:, cut], low[:, cut], samples)


def product_part(update, tiles, carry, name):
    flops = 384 * update.shape[1] * carry.shape[1]
    arrays = (update, *tiles, carry)
    return call(product_body, name, [(carry.shape, F32)], (), arrays, flops)[0]


def fused_body(sizes, which, table, lefts, points, scales, update, carry, out):
    samples, width = carry.shape
    terms = two_parts(update[...])
    tile = math.gcd(width, 512)

    def one_tile(at, _):
        right = right_of(sizes, which, table, points, scales, at, tile // GROUP)
        here = pl.ds(pl.multiple_of(at * tile, tile), tile)
        out[:, here] = carry[:, here] - dots(terms, *tiles_of(lefts[0], right), samples)
        return 0

    loop(width // tile, one_tile, 0)


def fused_part(sizes, which, table, lefts, points, scales, update, carry, name, after=()):
    return call(
        functools.partial(fused_body, sizes, which),
        name,
        [(carry.shape, F32)],
        (table,),
        (lefts, points, scales, update, carry),
        1600 * lefts.shape[1] * carry.shape[1],
        after,
        limit=12,
    )[0]


def arrange_body(sizes, layout, table, others, update, *refs):
    *pieces, out = refs
    for which, piece in zip(layout, pieces):
        source = others if isinstance(which, Other) else table
        for k in range(which.count):
            group = which.at(sizes, source, k)
            cut = group_cut(lax.rem(group, sizes.own))
            out[group // sizes.own, :, cut] = piece[:, k * GROUP : (k + 1) * GROUP]
    for j in range(sizes.rows):
        owner, inside = row_group(sizes, table, 0, j)

        @pl.when(owner == lax.axis_index("narrow"))
        def _():
            cut = group_cut(lax.rem(inside, sizes.own))
            diagonal = update[:, j * GROUP : (j + 1) * GROUP]
            out[inside // sizes.own, :, cut] -= NOISE_VAR * diagonal


def arrange_part(sizes, layout, table, others, update, pieces, after):
    shape = (sizes.shard // sizes.own, update.shape[0], sizes.own * GROUP)
    return call(
        functools.partial(arrange_body, sizes, layout),
        "arrange",
        [(shape, F32)],
        (table, others),
        (update, *pieces),
        1e8,
        after,
    )[0]


def last_body(sizes, side, table, update, arranged, *refs):
    *tiles, out = refs
    samples = update.shape[0]
    terms = two_parts(update[...])
    core = core_of(side)
    width = sizes.own * GROUP
    tile = math.gcd(width, 256)
    each = out.shape[0] * 2 // len(tiles)
    for part in range(out.shape[0]):
        high, low = tiles[2 * (part // each)], tiles[2 * (part // each) + 1]
        for begin in range(0, width, tile):
            base = (part % each) * width + begin
            cut, here = slice(base, base + tile), slice(begin, begin + tile)
            value = dots(terms, high[:, cut], low[:, cut], samples)
            out[part, :, here] = arranged[2 * part + core, :, here] - value
    for j in range(sizes.rows):
        owner, inside = row_group(sizes, table, 1, j)
        part = inside // sizes.own

        @pl.when((owner == lax.axis_index("narrow")) & (lax.rem(part, 2) == core))
        def _():
            cut = group_cut(lax.rem(inside, sizes.own))
            out[part // 2, :, cut] -= NOISE_VAR * update[:, j * GROUP : (j + 1) * GROUP]


def last_part(sizes, side, table, update, arranged, tiles, name):
    parts, samples, width = arranged.shape
    return call(
        functools.partial(last_body, sizes, side),
        name,
        [((parts // 2, samples, width), F32)],
        (table,),
        (update, arranged, *tiles),
        384 * update.shape[1] * parts * width // 2,
    )[0]


def exchange(value, axis, mask):
    count = lax.axis_size(axis)
    return lax.ppermute(value, axis, [(i, i ^ mask) for i in range(count)])


def butterfly(pair, axis, masks, windows, name):
    steps = list(zip(masks, masks[1:] + masks[:1]))
    for index, (one, two) in enumerate(steps):
        got = exchange(pair[0], axis, one), exchange(pair[1], axis, two)
        beside = windows[index](pair[0]) if index < len(windows) else []
        last = index == len(steps) - 1
        pair = add(pair, got, 1 if last else 2, beside, f"{name}_{index}")
    return pair[0]


def sum_wide(theirs, mine, windows, name):
    count = lax.axis_size("wide")
    pair = add((mine,), (exchange(theirs, "wide", 1),), 2, (), f"{name}_core")
    masks = [1 << bit for bit in range(1, count.bit_length() - 1)]
    return butterfly(pair, "wide", masks, windows, name)


def narrow_masks():
    return [(2 << bit) - 1 for bit in range(lax.axis_size("narrow").bit_length() - 1)]


def sum_narrow(value, windows, name):
    rows = value.shape[0] // 2
    return butterfly((value[:rows], value[rows:]), "narrow", narrow_masks(), windows, name)


def pick_body(mine, got, *outs):
    chip = lax.axis_index("wide") // 2
    for mask, out in enumerate(outs):
        out[...] = mine[chip ^ mask] + got[chip ^ mask]


def scatter_wide(theirs, mine):
    parts, *shape = mine.shape
    got = exchange(theirs, "wide", 1)
    shapes = [(tuple(shape), F32)] * parts
    own, *sent = call(pick_body, "pick", shapes, (), (mine, got), 1e8)
    return sum((exchange(part, "wide", 2 * mask) for mask, part in enumerate(sent, 1)), own)


def other_groups(table, sizes):
    narrow = lax.axis_index("narrow")
    used = lax.dynamic_slice_in_dim(table, narrow * sizes.share, sizes.share, 1).reshape(-1)
    used = used - narrow * sizes.shard
    ids = jnp.arange(sizes.shard, dtype=jnp.int32)
    free = ~jnp.any(ids[:, None] == used[None, :], axis=1)
    before = (ids[None, :] < ids[:, None]) & free[None, :]
    spot = jnp.sum(before.astype(jnp.int32), axis=1)
    slots = jnp.arange(sizes.shard - BLOCKS * sizes.share, dtype=jnp.int32)
    hit = (spot[None, :] == slots[:, None]) & free[None, :]
    return jnp.sum(jnp.where(hit, ids[None, :], 0), axis=1).astype(jnp.int32)


def on_device(
    all_features,
    points,
    scales,
    frequencies,
    phases,
    feature_weights,
    targets,
    noise,
    inverses,
    groups,
):
    wide_count, narrow_count = lax.axis_size("wide"), lax.axis_size("narrow")
    shard_groups = points.shape[1] // GROUP
    sizes = Sizes(
        shard_groups,
        groups.shape[1] // narrow_count,
        shard_groups // wide_count,
        groups.shape[1] // wide_count,
    )
    half = sizes.share // 2
    factor = math.sqrt(2.0 / all_features)
    targets, phases, scales = targets[None, :], phases[None, :], scales[:, None]
    left_over = sizes.shard - BLOCKS * sizes.share
    others = other_groups(groups, sizes) if left_over else groups

    arrays = (frequencies, phases, points, feature_weights, targets, noise)
    halves_0 = [Block(0, side, 0, half) for side in range(2)]
    halves_1 = [Block(1, side, 0, half) for side in range(2)]
    first_theirs, left, picked = prior_first(sizes, halves_0[0], factor, groups, arrays)
    shared = (left, feature_weights, points, targets, noise)
    first_mine = prior_part(
        sizes, halves_0[1], factor, groups, shared, "prior_mine", cost=2300
    )
    flat = picked.reshape(-1, picked.shape[2])

    def row_step(index, after):
        got = exchange(row_sums[-1], "narrow", narrow_masks()[index])
        row_sums.extend(add((row_sums[-1],), (got,), 1, (after,), f"rows_{index}"))

    row_sums = [flat]
    row_step(0, first_mine)

    piece = math.gcd(half, 4)
    pieces = [Block(1, side, begin, piece) for side in range(2) for begin in range(0, half, piece)]
    later = {}

    def prior_beside(chosen, extra, cost):
        def run(after):
            made = []
            for which in chosen:
                name = f"prior_{which.side}_{which.begin}"
                later[which] = prior_part(
                    sizes, which, factor, groups, shared, name, (after,), cost
                )
                made.append(later[which])
            return made + extra(after, made)

        return run

    def weights(mine, block, windows):
        theirs = exchange(mine, "wide", 1)
        part = inverse_part(mine, inverses, block, 1, (), f"inverse_{block}_mine")
        part = inverse_part(theirs, inverses, block, 0, (part,), f"inverse_{block}_theirs")
        return sum_narrow(part, windows, f"narrow_{block}")

    shares = [pieces[k::4] if len(pieces) > 4 else pieces[k : k + 1] for k in range(4)]
    lefts, tiles_0 = [], []

    def rows_beside(after, made):
        for index in range(1, len(narrow_masks())):
            row_step(index, made[-1])
        return row_sums[-1:]

    def lefts_beside(after, made):
        lefts.append(lefts_part(row_sums[-1].reshape(picked.shape), scales, (made[-1],)))
        return lefts

    def tiles_0_beside(side):
        def run(after, made):
            name = f"tiles_0_{side}"
            tiles_0.append(
                tiles_part(
                    sizes, halves_1[side], 0, groups, lefts[0], points, scales, name, (after,)
                )
            )
            return list(tiles_0[-1])

        return run

    extras = [rows_beside, lefts_beside, tiles_0_beside(0), tiles_0_beside(1)]
    costs = [2300, 2300, 400, 400]
    beside = [prior_beside(*terms) for terms in zip(shares, extras, costs)]
    whole = sum_wide(first_theirs, first_mine, beside[:2], "wide_0")
    update = weights(whole, 0, beside[2:])
    carries = [
        jnp.concatenate([later[which] for which in pieces if which.side == side], 1)
        for side in range(2)
    ]
    rest = [Other(begin, piece) for begin in range(0, left_over, piece)]
    rest_prior = [
        prior_part(sizes, which, factor, others, shared, f"prior_rest_{which.begin}")
        for which in rest
    ]
    tiles = functools.partial(tiles_part, sizes, lefts=lefts[0], points=points, scales=scales)
    fused = functools.partial(
        fused_part, sizes, lefts=lefts[0], points=points, scales=scales, update=update
    )
    following = [
        product_part(update, tiles_0[side], carries[side], f"product_0_{side}") for side in range(2)
    ]
    own_pieces = []

    def own_beside(side, carry):
        def run(after):
            name = f"fused_{side}"
            made = fused(halves_0[side], table=groups, carry=carry, name=name, after=(after,))
            own_pieces.append(made)
            return [made]

        return run

    windows = [own_beside(0, first_theirs), own_beside(1, first_mine)]
    whole = sum_wide(*following, windows, "wide_1")
    rest_pieces = [
        fused(which, table=others, carry=carry, name=f"fused_rest_{which.begin}")
        for which, carry in zip(rest, rest_prior)
    ]
    each = max(1, 8 // sizes.own)
    ahead = [[], []]
    arranged = []

    def ahead_beside(side):
        def run(after):
            for begin in range(0, wide_count // 2, each):
                ahead[side] += tiles(
                    Natural(side, begin, each * sizes.own),
                    block=1,
                    table=groups,
                    name=f"tiles_1_{side}_{begin}",
                    after=(after,),
                )
            made = list(ahead[side])
            if side:
                layout = [*halves_0, *halves_1, *rest]
                parts = [*own_pieces, *following, *rest_pieces]
                arranged.append(
                    arrange_part(sizes, layout, groups, others, update, parts, (after,))
                )
                made += arranged
            return made

        return run

    update_1 = weights(whole, 1, [ahead_beside(0), ahead_beside(1)])
    theirs, mine = (
        last_part(sizes, side, groups, update_1, arranged[0], ahead[side], f"last_{side}")
        for side in range(2)
    )
    return scatter_wide(theirs, mine), jnp.stack([update, update_1])


def solution(mesh):
    in_specs = (
        P(None, "narrow"),
        P(),
        P(None, "wide"),
        P("wide"),
        P(None, "wide"),
        P(("narrow", "wide")),
        P(None, ("narrow", "wide")),
        P(None, "wide", "narrow"),
        P(),
    )
    out_specs = (P(None, ("narrow", "wide")), P(None, None, "wide"))

    def run(points, scales, frequencies, *others):
        return jax.shard_map(
            functools.partial(on_device, frequencies.shape[1]),
            mesh=mesh,
            in_specs=in_specs,
            out_specs=out_specs,
            check_vma=False,
        )(points, scales, frequencies, *others)

    return run
```

profile of v0, /device:TPU:0, one launch (start us, length us, event | category | flops | bytes accessed | tf_op | source)
XLA Modules:
  0.0 120.1 jit_solution(17862395796681636633)
XLA Ops:
  0.7 11.9 %prior_first.1 = (f32[64,1024]{1,0:T(8,128)}, bf16[4096,64]{1,0:T(8,128)(2,1)}, f32[2,8,1024]{2,1,0:T(8,128)}) custom-call(s32[2,64]{1,0:T(2,128)} %refs_0_.33, f32[8,4096]{1,0:T(8,128)} %refs_1_.6, f32[1,4096]{1,0:T(1,128)} %bitcast.21, f32[8,4096]{1,0:T(8,128)} %refs_2_.25, bf16[64,4096]{1,0:T(8,128)(2,1)} %refs_2_.18, f32[1,512]{1,0:T(1,128)} %bitcast.14, ...), custom_call_target="tpu_custom_call" | custom-call | flops 9646899200 | tf_op jit(solution)/shard_map/prior_first/pallas_call | solution.py:139
  13.1 2.6 %collective-permute-start.3 = (f32[16,1024]{1,0:T(8,128)}, f32[16,1024]{1,0:T(8,128)S(1)}, u32[]{:S(2)}, u32[]{:S(2)}) collective-permute-start(f32[16,1024]{1,0:T(8,128)} %bitcast.12), channel_id=1, source_target_pairs={{0,1},{1,0},{2,3},{3,2},{4,5},{5,4},{6,7},{7,6},{8,9},{9,8},{10,11... | collective-permute-start | bytes 196616 | tf_op jit(solution)/shard_map/ppermute | solution.py:488
  17.0 8.9 %prior_mine.1.refs_0_.refs_2_.refs_5_ = f32[64,1024]{1,0:T(8,128)S(1)} custom-call(s32[2,64]{1,0:T(2,128)S(1)} %copy-done.1, bf16[4096,64]{1,0:T(8,128)(2,1)S(1)} %copy-done.7, bf16[64,4096]{1,0:T(8,128)(2,1)S(1)} %copy-done.2, f32[8,4096]{1,0:T(8,128)S(1)} %copy-done.5, f32[1,512]{1,0:T(1,128)S(1)} %bitcast.15, f32[64,512]{1,0:T(8,128)S(1)} %copy-done.4), custom_call_target="tpu_custom_call" | custom-call | flops 9646899200 | tf_op jit(solution)/shard_map/prior_mine/pallas_call | solution.py:139
  26.0 2.5 %collective-permute-start.4 = (f32[16,1024]{1,0:T(8,128)S(1)}, f32[16,1024]{1,0:T(8,128)S(1)}, u32[]{:S(2)}, u32[]{:S(2)}) collective-permute-start(f32[16,1024]{1,0:T(8,128)S(1)} %rows_0.1.refs_0_), channel_id=1, source_target_pairs={{0,3},{1,2},{2,1},{3,0},{4,7},{5,6},{6,5},{7,4},{8,11},{9,10},{10,... | collective-permute-start | bytes 196616 | tf_op jit(solution)/shard_map/ppermute | solution.py:488
  28.5 1.6 %collective-permute-start.1 = (f32[32,1024]{1,0:T(8,128)S(1)}, f32[32,1024]{1,0:T(8,128)S(1)}, u32[]{:S(2)}, u32[]{:S(2)}) collective-permute-start(f32[32,1024]{1,0:T(8,128)S(1)} %get-tuple-element.35.refs_6_.refs_0_), channel_id=1, source_target_pairs={{0,8},{4,12},{8,0},{12,4},{16,24},{20,28},{24,16},{28,20},{1,9},{5... | collective-permute-start | bytes 393224 | tf_op jit(solution)/shard_map/ppermute | solution.py:488
  30.1 1.5 %collective-permute-start.2 = (f32[32,1024]{1,0:T(8,128)S(1)}, f32[32,1024]{1,0:T(8,128)S(1)}, u32[]{:S(2)}, u32[]{:S(2)}) collective-permute-start(f32[32,1024]{1,0:T(8,128)S(1)} %get-tuple-element.36.refs_1_), channel_id=1, source_target_pairs={{0,16},{4,20},{8,24},{12,28},{16,0},{20,4},{24,8},{28,12},{1,17},{... | collective-permute-start | bytes 393224 | tf_op jit(solution)/shard_map/ppermute | solution.py:488
  31.6 4.7 %prior_0_0.1.refs_2_.refs_4_ = f32[64,512]{1,0:T(8,128)S(1)} custom-call(s32[2,64]{1,0:T(2,128)S(1)} %copy-done.1, bf16[4096,64]{1,0:T(8,128)(2,1)S(1)} %copy-done.8, bf16[64,4096]{1,0:T(8,128)(2,1)S(1)} %copy-done.2, f32[8,4096]{1,0:T(8,128)S(1)} %copy-done.5, f32[1,512]{1,0:T(1,128)S(1)} %bitcast.16, f32[64,512]{1,0:T(8,128)S(1)} %copy-done.4, ...), custom_call_target="tpu_custom_call" | custom-call | flops 4823449600 | tf_op jit(solution)/shard_map/prior_0_0/pallas_call | solution.py:139
  37.6 4.9 %prior_0_4.1.refs_2_.refs_4_ = f32[64,512]{1,0:T(8,128)S(1)} custom-call(s32[2,64]{1,0:T(2,128)S(1)} %copy-done.1, bf16[4096,64]{1,0:T(8,128)(2,1)S(1)} %copy-done.8, bf16[64,4096]{1,0:T(8,128)(2,1)S(1)} %copy-done.2, f32[8,4096]{1,0:T(8,128)S(1)} %copy-done.5, f32[1,512]{1,0:T(1,128)S(1)} %bitcast.17, f32[64,512]{1,0:T(8,128)S(1)} %copy-done.4, ...), custom_call_target="tpu_custom_call" | custom-call | flops 4823449600 | tf_op jit(solution)/shard_map/prior_0_4/pallas_call | solution.py:139
  43.1 1.5 %inverse_0_mine.1.refs_2_ = f32[64,1024]{1,0:T(8,128)S(1)} custom-call(f32[64,1024]{1,0:T(8,128)S(1)} %wide_0_1.1.refs_0_, f32[2,1024,2048]{2,1,0:T(8,128)S(1)} %bitcast.8), custom_call_target="tpu_custom_call" | custom-call | flops 536870912 | tf_op jit(solution)/shard_map/inverse_0_mine/pallas_call | solution.py:139
  44.5 1.5 %inverse_0_theirs.1 = f32[64,1024]{1,0:T(8,128)S(1)} custom-call(f32[64,1024]{1,0:T(8,128)S(1)} %collective-permute-done.7.refs_0_, f32[2,1024,2048]{2,1,0:T(8,128)S(1)} %bitcast.8, f32[64,1024]{1,0:T(8,128)S(1)} %inverse_0_mine.1.refs_2_), custom_call_target="tpu_custom_call" | custom-call | flops 536870912 | tf_op jit(solution)/shard_map/inverse_0_theirs/pallas_call | solution.py:139
  47.7 3.0 %tiles_0_0.1 = (bf16[1024,1024]{1,0:T(8,128)(2,1)S(1)}, bf16[1024,1024]{1,0:T(8,128)(2,1)S(1)}) custom-call(s32[2,64]{1,0:T(2,128)S(1)} %copy-done.1, bf16[2,1024,64]{2,1,0:T(8,128)(2,1)S(1)} %lefts.1.refs_5_.refs_1_, f32[8,4096]{1,0:T(8,128)S(1)} %copy-done.5, f32[8,1]{1,0:T(8,128)S(1)} %copy.11.refs_1_.refs_3_, ...), custom_call_target="tpu_custom_call" | custom-call | flops 314572800 | tf_op jit(solution)/shard_map/tiles_0_0/pallas_call | solution.py:139
  50.7 4.7 %prior_1_0.1.refs_4_ = f32[64,512]{1,0:T(8,128)S(1)} custom-call(s32[2,64]{1,0:T(2,128)S(1)} %copy-done.1, bf16[4096,64]{1,0:T(8,128)(2,1)S(1)} %copy-done.8, bf16[64,4096]{1,0:T(8,128)(2,1)S(1)} %copy-done.2, f32[8,4096]{1,0:T(8,128)S(1)} %copy-done.5, f32[1,512]{1,0:T(1,128)S(1)} %bitcast.18, f32[64,512]{1,0:T(8,128)S(1)} %copy-done.4, ...), custom_call_target="tpu_custom_call" | custom-call | flops 838860800 | tf_op jit(solution)/shard_map/prior_1_0/pallas_call | solution.py:139
  55.5 3.0 %collective-permute-start.10 = (f32[32,1024]{1,0:T(8,128)S(1)}, f32[32,1024]{1,0:T(8,128)S(1)}, u32[]{:S(2)}, u32[]{:S(2)}) collective-permute-start(f32[32,1024]{1,0:T(8,128)S(1)} %get-tuple-element.42.refs_6_.refs_4_.refs_0_), channel_id=1, source_target_pairs={{0,3},{1,2},{2,1},{3,0},{4,7},{5,6},{6,5},{7,4},{8,11},{9,10},{10,... | collective-permute-start | bytes 393224 | tf_op jit(solution)/shard_map/ppermute | solution.py:488
  58.5 3.0 %tiles_0_1.1 = (bf16[1024,1024]{1,0:T(8,128)(2,1)S(1)}, bf16[1024,1024]{1,0:T(8,128)(2,1)S(1)}) custom-call(s32[2,64]{1,0:T(2,128)S(1)} %copy-done.1, bf16[2,1024,64]{2,1,0:T(8,128)(2,1)S(1)} %lefts.1.refs_5_.refs_1_, f32[8,4096]{1,0:T(8,128)S(1)} %copy-done.5, f32[8,1]{1,0:T(8,128)S(1)} %copy.11.refs_1_.refs_3_, ...), custom_call_target="tpu_custom_call" | custom-call | flops 314572800 | tf_op jit(solution)/shard_map/tiles_0_1/pallas_call | solution.py:139
  61.6 4.9 %prior_1_4.1.refs_4_ = f32[64,512]{1,0:T(8,128)S(1)} custom-call(s32[2,64]{1,0:T(2,128)S(1)} %copy-done.1, bf16[4096,64]{1,0:T(8,128)(2,1)S(1)} %copy-done.8, bf16[64,4096]{1,0:T(8,128)(2,1)S(1)} %copy-done.2, f32[8,4096]{1,0:T(8,128)S(1)} %copy-done.5, f32[1,512]{1,0:T(1,128)S(1)} %bitcast.19, f32[64,512]{1,0:T(8,128)S(1)} %copy-done.4, ...), custom_call_target="tpu_custom_call" | custom-call | flops 838860800 | tf_op jit(solution)/shard_map/prior_1_4/pallas_call | solution.py:139
  69.0 1.5 %collective-permute-start.13 = (f32[32,1024]{1,0:T(8,128)S(1)}, f32[32,1024]{1,0:T(8,128)S(1)}, u32[]{:S(2)}, u32[]{:S(2)}) collective-permute-start(f32[32,1024]{1,0:T(8,128)S(1)} %get-tuple-element.46.refs_6_.refs_0_), channel_id=1, source_target_pairs={{0,8},{4,12},{8,0},{12,4},{16,24},{20,28},{24,16},{28,20},{1,9},{5... | collective-permute-start | bytes 393224 | tf_op jit(solution)/shard_map/ppermute | solution.py:488
  70.5 1.5 %collective-permute-start.14 = (f32[32,1024]{1,0:T(8,128)S(1)}, f32[32,1024]{1,0:T(8,128)S(1)}, u32[]{:S(2)}, u32[]{:S(2)}) collective-permute-start(f32[32,1024]{1,0:T(8,128)S(1)} %get-tuple-element.47.refs_1_), channel_id=1, source_target_pairs={{0,16},{4,20},{8,24},{12,28},{16,0},{20,4},{24,8},{28,12},{1,17},{... | collective-permute-start | bytes 393224 | tf_op jit(solution)/shard_map/ppermute | solution.py:488
  72.1 3.6 %fused_0.1.refs_4_.refs_3_ = f32[64,1024]{1,0:T(8,128)S(1)} custom-call(s32[2,64]{1,0:T(2,128)S(1)} %copy-done.1, bf16[2,1024,64]{2,1,0:T(8,128)(2,1)S(1)} %lefts.1.refs_5_.refs_1_, f32[8,4096]{1,0:T(8,128)S(1)} %copy-done.5, f32[8,1]{1,0:T(8,128)S(1)} %copy.11.refs_1_.refs_3_, f32[64,1024]{1,0:T(8,128)S(1)} %narrow_0_1.1.refs_0_.refs_4_.refs_2_, ...), custom_call_target="tpu_custom_call" | custom-call | flops 1677721600 | tf_op jit(solution)/shard_map/fused_0/pallas_call | solution.py:139
  75.8 1.6 %collective-permute-start.15 = (f32[32,1024]{1,0:T(8,128)S(1)}, f32[32,1024]{1,0:T(8,128)S(1)}, u32[]{:S(2)}, u32[]{:S(2)}) collective-permute-start(f32[32,1024]{1,0:T(8,128)S(1)} %get-tuple-element.48.refs_6_.refs_0_), channel_id=1, source_target_pairs={{0,16},{4,20},{8,24},{12,28},{16,0},{20,4},{24,8},{28,12},{1,17},{... | collective-permute-start | bytes 393224 | tf_op jit(solution)/shard_map/ppermute | solution.py:488
  78.0 3.6 %fused_1.1.refs_4_ = f32[64,1024]{1,0:T(8,128)S(1)} custom-call(s32[2,64]{1,0:T(2,128)S(1)} %copy-done.1, bf16[2,1024,64]{2,1,0:T(8,128)(2,1)S(1)} %lefts.1.refs_5_.refs_1_, f32[8,4096]{1,0:T(8,128)S(1)} %copy-done.5, f32[8,1]{1,0:T(8,128)S(1)} %copy.11.refs_1_.refs_3_, f32[64,1024]{1,0:T(8,128)S(1)} %narrow_0_1.1.refs_0_.refs_4_.refs_2_, ...), custom_call_target="tpu_custom_call" | custom-call | flops 1677721600 | tf_op jit(solution)/shard_map/fused_1/pallas_call | solution.py:139
  84.0 1.5 %inverse_1_theirs.1 = f32[64,1024]{1,0:T(8,128)S(1)} custom-call(f32[64,1024]{1,0:T(8,128)S(1)} %collective-permute-done.17.refs_0_, f32[2,1024,2048]{2,1,0:T(8,128)S(1)} %bitcast.8, f32[64,1024]{1,0:T(8,128)S(1)} %inverse_1_mine.1.refs_2_), custom_call_target="tpu_custom_call" | custom-call | flops 536870912 | tf_op jit(solution)/shard_map/inverse_1_theirs/pallas_call | solution.py:139
  85.5 2.1 %collective-permute-start.18 = (f32[32,1024]{1,0:T(8,128)S(1)}, f32[32,1024]{1,0:T(8,128)S(1)}, u32[]{:S(2)}, u32[]{:S(2)}) collective-permute-start(f32[32,1024]{1,0:T(8,128)S(1)} %get-tuple-element.65.refs_4_.refs_0_), channel_id=1, source_target_pairs={{0,1},{1,0},{2,3},{3,2},{4,5},{5,4},{6,7},{7,6},{8,9},{9,8},{10,11... | collective-permute-start | bytes 393224 | tf_op jit(solution)/shard_map/ppermute | solution.py:488
  88.6 3.0 %tiles_1_0_2.1 = (bf16[1024,1024]{1,0:T(8,128)(2,1)S(1)}, bf16[1024,1024]{1,0:T(8,128)(2,1)S(1)}) custom-call(s32[2,64]{1,0:T(2,128)S(1)} %copy-done.1, bf16[2,1024,64]{2,1,0:T(8,128)(2,1)S(1)} %lefts.1.refs_5_.refs_1_, f32[8,4096]{1,0:T(8,128)S(1)} %copy-done.5, f32[8,1]{1,0:T(8,128)S(1)} %copy.11.refs_1_.refs_3_, ...), custom_call_target="tpu_custom_call" | custom-call | flops 314572800 | tf_op jit(solution)/shard_map/tiles_1_0_2/pallas_call | solution.py:139
  91.6 3.0 %tiles_1_0_0.1 = (bf16[1024,1024]{1,0:T(8,128)(2,1)S(1)}, bf16[1024,1024]{1,0:T(8,128)(2,1)S(1)}) custom-call(s32[2,64]{1,0:T(2,128)S(1)} %copy-done.1, bf16[2,1024,64]{2,1,0:T(8,128)(2,1)S(1)} %lefts.1.refs_5_.refs_1_, f32[8,4096]{1,0:T(8,128)S(1)} %copy-done.5, f32[8,1]{1,0:T(8,128)S(1)} %copy.11.refs_1_.refs_3_, ...), custom_call_target="tpu_custom_call" | custom-call | flops 314572800 | tf_op jit(solution)/shard_map/tiles_1_0_0/pallas_call | solution.py:139
  95.3 2.8 %collective-permute-start.20 = (f32[32,1024]{1,0:T(8,128)S(1)}, f32[32,1024]{1,0:T(8,128)S(1)}, u32[]{:S(2)}, u32[]{:S(2)}) collective-permute-start(f32[32,1024]{1,0:T(8,128)S(1)} %get-tuple-element.54.refs_4_.refs_7_.refs_0_), channel_id=1, source_target_pairs={{0,3},{1,2},{2,1},{3,0},{4,7},{5,6},{6,5},{7,4},{8,11},{9,10},{10,... | collective-permute-start | bytes 393224 | tf_op jit(solution)/shard_map/ppermute | solution.py:488
  99.5 3.0 %tiles_1_1_2.1 = (bf16[1024,1024]{1,0:T(8,128)(2,1)S(1)}, bf16[1024,1024]{1,0:T(8,128)(2,1)S(1)}) custom-call(s32[2,64]{1,0:T(2,128)S(1)} %copy-done.1, bf16[2,1024,64]{2,1,0:T(8,128)(2,1)S(1)} %lefts.1.refs_5_.refs_1_, f32[8,4096]{1,0:T(8,128)S(1)} %copy-done.5, f32[8,1]{1,0:T(8,128)S(1)} %copy.11.refs_1_.refs_3_, ...), custom_call_target="tpu_custom_call" | custom-call | flops 314572800 | tf_op jit(solution)/shard_map/tiles_1_1_2/pallas_call | solution.py:139
  102.6 3.0 %tiles_1_1_0.1 = (bf16[1024,1024]{1,0:T(8,128)(2,1)S(1)}, bf16[1024,1024]{1,0:T(8,128)(2,1)S(1)}) custom-call(s32[2,64]{1,0:T(2,128)S(1)} %copy-done.1, bf16[2,1024,64]{2,1,0:T(8,128)(2,1)S(1)} %lefts.1.refs_5_.refs_1_, f32[8,4096]{1,0:T(8,128)S(1)} %copy-done.5, f32[8,1]{1,0:T(8,128)S(1)} %copy.11.refs_1_.refs_3_, ...), custom_call_target="tpu_custom_call" | custom-call | flops 314572800 | tf_op jit(solution)/shard_map/tiles_1_1_0/pallas_call | solution.py:139
  105.7 2.2 %last_0.1 = f32[4,64,512]{2,1,0:T(8,128)S(1)} custom-call(s32[2,64]{1,0:T(2,128)S(1)} %copy-done.1, f32[64,1024]{1,0:T(8,128)S(1)} %narrow_1_1.1.refs_1_, f32[8,64,512]{2,1,0:T(8,128)S(1)} %arrange.1.refs_8_.refs_2_, bf16[1024,1024]{1,0:T(8,128)(2,1)S(1)} %get-tuple-element.50.refs_4_.refs_3_, bf16[1024,1024]{1,0:T(8,128)(2,1)S(1)} %get-tuple-element.51.refs_5_.refs_4_, ...), custom_call_target="tpu_custom_call" | custom-call | flops 805306368 | tf_op jit(solution)/shard_map/last_0/pallas_call | solution.py:139
  108.0 2.2 %last_1.1.refs_0_ = f32[4,64,512]{2,1,0:T(8,128)S(1)} custom-call(s32[2,64]{1,0:T(2,128)S(1)} %copy-done.1, f32[64,1024]{1,0:T(8,128)S(1)} %narrow_1_1.1.refs_1_, f32[8,64,512]{2,1,0:T(8,128)S(1)} %arrange.1.refs_8_.refs_2_, bf16[1024,1024]{1,0:T(8,128)(2,1)S(1)} %get-tuple-element.56.refs_4_.refs_3_, ...), custom_call_target="tpu_custom_call" | custom-call | flops 805306368 | tf_op jit(solution)/shard_map/last_1/pallas_call | solution.py:139
  111.4 2.5 %collective-permute-start.25 = (f32[64,512]{1,0:T(8,128)S(1)}, f32[64,512]{1,0:T(8,128)S(1)}, u32[]{:S(2)}, u32[]{:S(2)}) collective-permute-start(f32[64,512]{1,0:T(8,128)S(1)} %get-tuple-element.63), channel_id=1, source_target_pairs={{0,24},{4,28},{8,16},{12,20},{16,8},{20,12},{24,0},{28,4},{1,25},{... | collective-permute-start | bytes 393224 | tf_op jit(solution)/shard_map/ppermute | solution.py:488
  114.7 2.0 %collective-permute-done.23 = f32[64,512]{1,0:T(8,128)S(1)} collective-permute-done((f32[64,512]{1,0:T(8,128)S(1)}, f32[64,512]{1,0:T(8,128)S(1)}, u32[]{:S(2)}, u32[]{:S(2)}) %collective-permute-start.23) | collective-permute-done | bytes 131104 | tf_op jit(solution)/shard_map/ppermute | solution.py:488
  116.7 2.7 %collective-permute-done.24 = f32[64,512]{1,0:T(8,128)S(1)} collective-permute-done((f32[64,512]{1,0:T(8,128)S(1)}, f32[64,512]{1,0:T(8,128)S(1)}, u32[]{:S(2)}, u32[]{:S(2)}) %collective-permute-start.24) | collective-permute-done | bytes 131104 | tf_op jit(solution)/shard_map/ppermute | solution.py:488
  (93 shorter events, 16.7 us)
Async XLA Ops:
  0.6 15.1 %copy-start.1 = (s32[2,64]{1,0:T(2,128)S(1)}, s32[2,64]{1,0:T(2,128)}, u32[]{:S(2)}) copy-start(s32[2,64]{1,0:T(2,128)} %refs_0_.33) | copy-start | bytes 1540
  0.6 15.1 %copy-start.2 = (bf16[64,4096]{1,0:T(8,128)(2,1)S(1)}, bf16[64,4096]{1,0:T(8,128)(2,1)}, u32[]{:S(2)}) copy-start(bf16[64,4096]{1,0:T(8,128)(2,1)} %refs_2_.18) | copy-start | bytes 1572868
  0.7 15.1 %copy-start.4 = (f32[64,512]{1,0:T(8,128)S(1)}, f32[64,512]{1,0:T(8,128)}, u32[]{:S(2)}) copy-start(f32[64,512]{1,0:T(8,128)} %refs_5_.9) | copy-start | bytes 393220
  0.7 15.1 %copy-start.5 = (f32[8,4096]{1,0:T(8,128)S(1)}, f32[8,4096]{1,0:T(8,128)}, u32[]{:S(2)}) copy-start(f32[8,4096]{1,0:T(8,128)} %refs_2_.25) | copy-start | bytes 393220
  0.7 15.1 %copy-start.6 = (f32[512]{0:T(512)S(1)}, f32[512]{0:T(512)}, u32[]{:S(2)}) copy-start(f32[512]{0:T(512)} %param.14) | copy-start | bytes 6148
  12.6 16.0 %collective-permute-start = (f32[64,1024]{1,0:T(8,128)}, f32[64,1024]{1,0:T(8,128)S(1)}, u32[]{:S(2)}, u32[]{:S(2)}) collective-permute-start(f32[64,1024]{1,0:T(8,128)} %get-tuple-element.34.refs_5_), channel_id=1, source_target_pairs={{0,4},{4,0},{8,12},{12,8},{16,20},{20,16},{24,28},{28,24},{1,5},{5... | collective-permute-start | bytes 786440 | tf_op jit(solution)/shard_map/ppermute | solution.py:488
  13.1 12.9 %collective-permute-start.3 = (f32[16,1024]{1,0:T(8,128)}, f32[16,1024]{1,0:T(8,128)S(1)}, u32[]{:S(2)}, u32[]{:S(2)}) collective-permute-start(f32[16,1024]{1,0:T(8,128)} %bitcast.12), channel_id=1, source_target_pairs={{0,1},{1,0},{2,3},{3,2},{4,5},{5,4},{6,7},{7,6},{8,9},{9,8},{10,11... | collective-permute-start | bytes 196616 | tf_op jit(solution)/shard_map/ppermute | solution.py:488
  17.0 14.7 %copy-start.8 = (bf16[4096,64]{1,0:T(8,128)(2,1)S(1)}, bf16[4096,64]{1,0:T(8,128)(2,1)}, u32[]{:S(2)}) copy-start(bf16[4096,64]{1,0:T(8,128)(2,1)} %get-tuple-element.33.refs_1_) | copy-start | bytes 1572868
  26.0 10.4 %collective-permute-start.4 = (f32[16,1024]{1,0:T(8,128)S(1)}, f32[16,1024]{1,0:T(8,128)S(1)}, u32[]{:S(2)}, u32[]{:S(2)}) collective-permute-start(f32[16,1024]{1,0:T(8,128)S(1)} %rows_0.1.refs_0_), channel_id=1, source_target_pairs={{0,3},{1,2},{2,1},{3,0},{4,7},{5,6},{6,5},{7,4},{8,11},{9,10},{10,... | collective-permute-start | bytes 196616 | tf_op jit(solution)/shard_map/ppermute | solution.py:488
  28.5 7.9 %collective-permute-start.1 = (f32[32,1024]{1,0:T(8,128)S(1)}, f32[32,1024]{1,0:T(8,128)S(1)}, u32[]{:S(2)}, u32[]{:S(2)}) collective-permute-start(f32[32,1024]{1,0:T(8,128)S(1)} %get-tuple-element.35.refs_6_.refs_0_), channel_id=1, source_target_pairs={{0,8},{4,12},{8,0},{12,4},{16,24},{20,28},{24,16},{28,20},{1,9},{5... | collective-permute-start | bytes 393224 | tf_op jit(solution)/shard_map/ppermute | solution.py:488
  30.1 6.3 %collective-permute-start.2 = (f32[32,1024]{1,0:T(8,128)S(1)}, f32[32,1024]{1,0:T(8,128)S(1)}, u32[]{:S(2)}, u32[]{:S(2)}) collective-permute-start(f32[32,1024]{1,0:T(8,128)S(1)} %get-tuple-element.36.refs_1_), channel_id=1, source_target_pairs={{0,16},{4,20},{8,24},{12,28},{16,0},{20,4},{24,8},{28,12},{1,17},{... | collective-permute-start | bytes 393224 | tf_op jit(solution)/shard_map/ppermute | solution.py:488
  36.5 6.4 %collective-permute-start.5 = (f32[32,1024]{1,0:T(8,128)S(1)}, f32[32,1024]{1,0:T(8,128)S(1)}, u32[]{:S(2)}, u32[]{:S(2)}) collective-permute-start(f32[32,1024]{1,0:T(8,128)S(1)} %get-tuple-element.38.refs_6_.refs_0_), channel_id=1, source_target_pairs={{0,16},{4,20},{8,24},{12,28},{16,0},{20,4},{24,8},{28,12},{1,17},{... | collective-permute-start | bytes 393224 | tf_op jit(solution)/shard_map/ppermute | solution.py:488
  37.1 5.8 %collective-permute-start.6 = (f32[32,1024]{1,0:T(8,128)S(1)}, f32[32,1024]{1,0:T(8,128)S(1)}, u32[]{:S(2)}, u32[]{:S(2)}) collective-permute-start(f32[32,1024]{1,0:T(8,128)S(1)} %get-tuple-element.39.refs_1_), channel_id=1, source_target_pairs={{0,8},{4,12},{8,0},{12,4},{16,24},{20,28},{24,16},{28,20},{1,9},{5... | collective-permute-start | bytes 393224 | tf_op jit(solution)/shard_map/ppermute | solution.py:488
  42.9 1.6 %collective-permute-start.7 = (f32[64,1024]{1,0:T(8,128)S(1)}, f32[64,1024]{1,0:T(8,128)S(1)}, u32[]{:S(2)}, u32[]{:S(2)}) collective-permute-start(f32[64,1024]{1,0:T(8,128)S(1)} %wide_0_1.1.refs_0_), channel_id=1, source_target_pairs={{0,4},{4,0},{8,12},{12,8},{16,20},{20,16},{24,28},{28,24},{1,5},{5... | collective-permute-start | bytes 786440 | tf_op jit(solution)/shard_map/ppermute | solution.py:488
  46.0 9.4 %collective-permute-start.8 = (f32[32,1024]{1,0:T(8,128)S(1)}, f32[32,1024]{1,0:T(8,128)S(1)}, u32[]{:S(2)}, u32[]{:S(2)}) collective-permute-start(f32[32,1024]{1,0:T(8,128)S(1)} %get-tuple-element.67.refs_6_.refs_4_.refs_0_), channel_id=1, source_target_pairs={{0,1},{1,0},{2,3},{3,2},{4,5},{5,4},{6,7},{7,6},{8,9},{9,8},{10,11... | collective-permute-start | bytes 393224 | tf_op jit(solution)/shard_map/ppermute | solution.py:488
  46.8 8.7 %collective-permute-start.9 = (f32[32,1024]{1,0:T(8,128)S(1)}, f32[32,1024]{1,0:T(8,128)S(1)}, u32[]{:S(2)}, u32[]{:S(2)}) collective-permute-start(f32[32,1024]{1,0:T(8,128)S(1)} %get-tuple-element.66.refs_1_), channel_id=1, source_target_pairs={{0,3},{1,2},{2,1},{3,0},{4,7},{5,6},{6,5},{7,4},{8,11},{9,10},{10,... | collective-permute-start | bytes 393224 | tf_op jit(solution)/shard_map/ppermute | solution.py:488
  55.5 11.0 %collective-permute-start.10 = (f32[32,1024]{1,0:T(8,128)S(1)}, f32[32,1024]{1,0:T(8,128)S(1)}, u32[]{:S(2)}, u32[]{:S(2)}) collective-permute-start(f32[32,1024]{1,0:T(8,128)S(1)} %get-tuple-element.42.refs_6_.refs_4_.refs_0_), channel_id=1, source_target_pairs={{0,3},{1,2},{2,1},{3,0},{4,7},{5,6},{6,5},{7,4},{8,11},{9,10},{10,... | collective-permute-start | bytes 393224 | tf_op jit(solution)/shard_map/ppermute | solution.py:488
  58.5 8.0 %collective-permute-start.11 = (f32[32,1024]{1,0:T(8,128)S(1)}, f32[32,1024]{1,0:T(8,128)S(1)}, u32[]{:S(2)}, u32[]{:S(2)}) collective-permute-start(f32[32,1024]{1,0:T(8,128)S(1)} %get-tuple-element.43.refs_1_), channel_id=1, source_target_pairs={{0,1},{1,0},{2,3},{3,2},{4,5},{5,4},{6,7},{7,6},{8,9},{9,8},{10,11... | collective-permute-start | bytes 393224 | tf_op jit(solution)/shard_map/ppermute | solution.py:488
  67.4 1.6 %collective-permute-start.12 = (f32[64,1024]{1,0:T(8,128)S(1)}, f32[64,1024]{1,0:T(8,128)S(1)}, u32[]{:S(2)}, u32[]{:S(2)}) collective-permute-start(f32[64,1024]{1,0:T(8,128)S(1)} %product_0_0.1.refs_5_), channel_id=1, source_target_pairs={{0,4},{4,0},{8,12},{12,8},{16,20},{20,16},{24,28},{28,24},{1,5},{5... | collective-permute-start | bytes 786440 | tf_op jit(solution)/shard_map/ppermute | solution.py:488
  69.0 6.7 %collective-permute-start.13 = (f32[32,1024]{1,0:T(8,128)S(1)}, f32[32,1024]{1,0:T(8,128)S(1)}, u32[]{:S(2)}, u32[]{:S(2)}) collective-permute-start(f32[32,1024]{1,0:T(8,128)S(1)} %get-tuple-element.46.refs_6_.refs_0_), channel_id=1, source_target_pairs={{0,8},{4,12},{8,0},{12,4},{16,24},{20,28},{24,16},{28,20},{1,9},{5... | collective-permute-start | bytes 393224 | tf_op jit(solution)/shard_map/ppermute | solution.py:488
  70.5 5.3 %collective-permute-start.14 = (f32[32,1024]{1,0:T(8,128)S(1)}, f32[32,1024]{1,0:T(8,128)S(1)}, u32[]{:S(2)}, u32[]{:S(2)}) collective-permute-start(f32[32,1024]{1,0:T(8,128)S(1)} %get-tuple-element.47.refs_1_), channel_id=1, source_target_pairs={{0,16},{4,20},{8,24},{12,28},{16,0},{20,4},{24,8},{28,12},{1,17},{... | collective-permute-start | bytes 393224 | tf_op jit(solution)/shard_map/ppermute | solution.py:488
  75.8 5.8 %collective-permute-start.15 = (f32[32,1024]{1,0:T(8,128)S(1)}, f32[32,1024]{1,0:T(8,128)S(1)}, u32[]{:S(2)}, u32[]{:S(2)}) collective-permute-start(f32[32,1024]{1,0:T(8,128)S(1)} %get-tuple-element.48.refs_6_.refs_0_), channel_id=1, source_target_pairs={{0,16},{4,20},{8,24},{12,28},{16,0},{20,4},{24,8},{28,12},{1,17},{... | collective-permute-start | bytes 393224 | tf_op jit(solution)/shard_map/ppermute | solution.py:488
  77.4 5.0 %collective-permute-start.16 = (f32[32,1024]{1,0:T(8,128)S(1)}, f32[32,1024]{1,0:T(8,128)S(1)}, u32[]{:S(2)}, u32[]{:S(2)}) collective-permute-start(f32[32,1024]{1,0:T(8,128)S(1)} %get-tuple-element.49.refs_1_), channel_id=1, source_target_pairs={{0,8},{4,12},{8,0},{12,4},{16,24},{20,28},{24,16},{28,20},{1,9},{5... | collective-permute-start | bytes 393224 | tf_op jit(solution)/shard_map/ppermute | solution.py:488
  82.4 1.6 %collective-permute-start.17 = (f32[64,1024]{1,0:T(8,128)S(1)}, f32[64,1024]{1,0:T(8,128)S(1)}, u32[]{:S(2)}, u32[]{:S(2)}) collective-permute-start(f32[64,1024]{1,0:T(8,128)S(1)} %wide_1_1.1.refs_0_), channel_id=1, source_target_pairs={{0,4},{4,0},{8,12},{12,8},{16,20},{20,16},{24,28},{28,24},{1,5},{5... | collective-permute-start | bytes 786440 | tf_op jit(solution)/shard_map/ppermute | solution.py:488
  85.5 9.1 %collective-permute-start.18 = (f32[32,1024]{1,0:T(8,128)S(1)}, f32[32,1024]{1,0:T(8,128)S(1)}, u32[]{:S(2)}, u32[]{:S(2)}) collective-permute-start(f32[32,1024]{1,0:T(8,128)S(1)} %get-tuple-element.65.refs_4_.refs_0_), channel_id=1, source_target_pairs={{0,1},{1,0},{2,3},{3,2},{4,5},{5,4},{6,7},{7,6},{8,9},{9,8},{10,11... | collective-permute-start | bytes 393224 | tf_op jit(solution)/shard_map/ppermute | solution.py:488
  87.6 7.7 %collective-permute-start.19 = (f32[32,1024]{1,0:T(8,128)S(1)}, f32[32,1024]{1,0:T(8,128)S(1)}, u32[]{:S(2)}, u32[]{:S(2)}) collective-permute-start(f32[32,1024]{1,0:T(8,128)S(1)} %get-tuple-element.64.refs_1_), channel_id=1, source_target_pairs={{0,3},{1,2},{2,1},{3,0},{4,7},{5,6},{6,5},{7,4},{8,11},{9,10},{10,... | collective-permute-start | bytes 393224 | tf_op jit(solution)/shard_map/ppermute | solution.py:488
  95.3 10.3 %collective-permute-start.20 = (f32[32,1024]{1,0:T(8,128)S(1)}, f32[32,1024]{1,0:T(8,128)S(1)}, u32[]{:S(2)}, u32[]{:S(2)}) collective-permute-start(f32[32,1024]{1,0:T(8,128)S(1)} %get-tuple-element.54.refs_4_.refs_7_.refs_0_), channel_id=1, source_target_pairs={{0,3},{1,2},{2,1},{3,0},{4,7},{5,6},{6,5},{7,4},{8,11},{9,10},{10,... | collective-permute-start | bytes 393224 | tf_op jit(solution)/shard_map/ppermute | solution.py:488
  98.2 7.5 %collective-permute-start.21 = (f32[32,1024]{1,0:T(8,128)S(1)}, f32[32,1024]{1,0:T(8,128)S(1)}, u32[]{:S(2)}, u32[]{:S(2)}) collective-permute-start(f32[32,1024]{1,0:T(8,128)S(1)} %get-tuple-element.55.refs_1_), channel_id=1, source_target_pairs={{0,1},{1,0},{2,3},{3,2},{4,5},{5,4},{6,7},{7,6},{8,9},{9,8},{10,11... | collective-permute-start | bytes 393224 | tf_op jit(solution)/shard_map/ppermute | solution.py:488
  107.9 2.3 %collective-permute-start.22 = (f32[4,64,512]{2,1,0:T(8,128)S(1)}, f32[4,64,512]{2,1,0:T(8,128)S(1)}, u32[]{:S(2)}, u32[]{:S(2)}) collective-permute-start(f32[4,64,512]{2,1,0:T(8,128)S(1)} %last_0.1), channel_id=1, source_target_pairs={{0,4},{4,0},{8,12},{12,8},{16,20},{20,16},{24,28},{28,24},{1,5},{5... | collective-permute-start | bytes 1572872 | tf_op jit(solution)/shard_map/ppermute | solution.py:488
  110.3 6.4 %collective-permute-start.23 = (f32[64,512]{1,0:T(8,128)S(1)}, f32[64,512]{1,0:T(8,128)S(1)}, u32[]{:S(2)}, u32[]{:S(2)}) collective-permute-start(f32[64,512]{1,0:T(8,128)S(1)} %get-tuple-element.61), channel_id=1, source_target_pairs={{0,8},{4,12},{8,0},{12,4},{16,24},{20,28},{24,16},{28,20},{1,9},{5... | collective-permute-start | bytes 393224 | tf_op jit(solution)/shard_map/ppermute | solution.py:488
  110.9 8.4 %collective-permute-start.24 = (f32[64,512]{1,0:T(8,128)S(1)}, f32[64,512]{1,0:T(8,128)S(1)}, u32[]{:S(2)}, u32[]{:S(2)}) collective-permute-start(f32[64,512]{1,0:T(8,128)S(1)} %get-tuple-element.62), channel_id=1, source_target_pairs={{0,16},{4,20},{8,24},{12,28},{16,0},{20,4},{24,8},{28,12},{1,17},{... | collective-permute-start | bytes 393224 | tf_op jit(solution)/shard_map/ppermute | solution.py:488
  111.4 8.0 %collective-permute-start.25 = (f32[64,512]{1,0:T(8,128)S(1)}, f32[64,512]{1,0:T(8,128)S(1)}, u32[]{:S(2)}, u32[]{:S(2)}) collective-permute-start(f32[64,512]{1,0:T(8,128)S(1)} %get-tuple-element.63), channel_id=1, source_target_pairs={{0,24},{4,28},{8,16},{12,20},{16,8},{20,12},{24,0},{28,4},{1,25},{... | collective-permute-start | bytes 393224 | tf_op jit(solution)/shard_map/ppermute | solution.py:488
  (8 other events, 58.5 us)
where the time goes:
time: 120 us
  Pallas kernels  79.5 us (66%)
  starting transfers between devices  29.5 us (25%)
  waiting for transfers between devices  7.02 us (6%)
  other arithmetic  1.57 us (1%)
  local copies, waits for them, and re-layouts  1.39 us (1%)
    pallas_call x37, Pallas kernels, call(): pl.pallas_call(run, out_shape=[jax.ShapeDtypeStruct(*shape) for shape in...  79.5 us
    ppermute x26, starting transfers between devices, exchange(): return lax.ppermute(value, axis, [(i, i ^ mask) for i in range(count)])  29.5 us
    ppermute x26, waiting for transfers between devices, exchange(): return lax.ppermute(value, axis, [(i, i ^ mask) for i in range(count)])  7.02 us
  transfers between devices with their start and end apart: 26, of which 7 were waited for; matrix products, arithmetic and copies ran while one was open for 1% of the time, Pallas kernels for 51%

commit v1 on v0

--- a/solution.py
+++ b/solution.py
@@ -155,23 +155,25 @@
 
 
 def prior_tiles(sizes, which, factor, table, left, fw, points, targets, noise, out):
-    features, width = left.shape[0], out.shape[1]
-    tile, chunk = math.gcd(width, 512), math.gcd(features, 2048)
+    chunk, width = left.shape[0], out.shape[1]
+    tile = math.gcd(width, 512)
     per = tile // GROUP
     ones = jnp.ones((1, tile), F32)
 
     def one_tile(at, _):
         groups = [which.at(sizes, table, at * per + k) for k in range(per)]
         coords = jnp.concatenate([group_of(points, group) for group in groups], 1)
-        right = right_terms(thirds(coords), stack_rows([ones] * 3)).astype(BF16)
+        right = right_terms(thirds(coords), stack_rows([ones] * 3))
 
         def one_chunk(index, total):
             cut = pl.ds(pl.multiple_of(index * chunk, chunk), chunk)
-            turns = jnp.dot(left[cut, :], right, preferred_element_type=F32)
+            sides = [jnp.where(index == side, right, 0.0) for side in range(2)]
+            both = jnp.concatenate(sides, 0).astype(BF16)
+            turns = jnp.dot(left[...], both, preferred_element_type=F32)
             values = cosine(turns).astype(BF16)
             return total + jnp.dot(fw[:, cut], values, preferred_element_type=F32)
 
-        total = loop(features // chunk, one_chunk, jnp.zeros((out.shape[0], tile), F32))
+        total = loop(2, one_chunk, jnp.zeros((out.shape[0], tile), F32))
         out[:, pl.ds(pl.multiple_of(at * tile, tile), tile)] = -factor * total
         for k, group in enumerate(groups):
 
@@ -197,16 +199,20 @@
     copies[0].wait()
     copies[1].wait()
     features = freq.shape[1]
-    step = math.gcd(features, 1024)
+    middle = features // 2
+    step = math.gcd(middle, 512)
 
     def one_step(index, _):
+        sides = []
+        for begin in (0, middle):
+            cut = pl.ds(pl.multiple_of(begin + index * step, step), step)
+            extra = stack_rows(thirds(phase[:, cut] * TO_TURNS))
+            sides.append(left_terms(thirds(freq[:, cut] * TO_TURNS), extra))
         cut = pl.ds(pl.multiple_of(index * step, step), step)
-        extra = stack_rows(thirds(phase[:, cut] * TO_TURNS))
-        terms = left_terms(thirds(freq[:, cut] * TO_TURNS), extra)
-        left[cut, :] = terms.T.astype(BF16)
+        left[cut, :] = jnp.concatenate(sides, 0).T.astype(BF16)
         return 0
 
-    loop(features // step, one_step, 0)
+    loop(middle // step, one_step, 0)
     copies[2].wait()
     for block in range(BLOCKS):
         for j in range(sizes.rows):
@@ -224,7 +230,7 @@
     width = which.count * GROUP
     shapes = [
         ((samples, width), F32),
-        ((features, 64), BF16),
+        ((features // 2, 128), BF16),
         ((BLOCKS, freq.shape[0], sizes.rows * GROUP), F32),
     ]
     scratch = [pltpu.VMEM(array.shape, array.dtype) for array in arrays]

time: 120 us -> 120 us (level)
  no operation moved by 1% of the time
where the time goes in v1:
time: 120 us
  Pallas kernels  79.3 us (66%)
  starting transfers between devices  29.4 us (24%)
  waiting for transfers between devices  7.02 us (6%)
  other arithmetic  1.57 us (1%)
  local copies, waits for them, and re-layouts  1.21 us (1%)
    pallas_call x37, Pallas kernels, call(): pl.pallas_call(run, out_shape=[jax.ShapeDtypeStruct(*shape) for shape in...  79.3 us
    ppermute x26, starting transfers between devices, exchange(): return lax.ppermute(value, axis, [(i, i ^ mask) for i in range(count)])  29.4 us
    ppermute x26, waiting for transfers between devices, exchange(): return lax.ppermute(value, axis, [(i, i ^ mask) for i in range(count)])  7.02 us
  transfers between devices with their start and end apart: 26, of which 7 were waited for; matrix products, arithmetic and copies ran while one was open for 1% of the time, Pallas kernels for 51%

profile of v1, /device:TPU:0, one launch (start us, length us, event | category | flops | bytes accessed | tf_op | source)
XLA Modules:
  0.0 119.7 jit_solution(7711507075699640305)
XLA Ops:
  0.7 11.6 %prior_first.1 = (f32[64,1024]{1,0:T(8,128)}, bf16[2048,128]{1,0:T(8,128)(2,1)}, f32[2,8,1024]{2,1,0:T(8,128)}) custom-call(s32[2,64]{1,0:T(2,128)} %refs_0_.33, f32[8,4096]{1,0:T(8,128)} %refs_1_.6, f32[1,4096]{1,0:T(1,128)} %bitcast.21, f32[8,4096]{1,0:T(8,128)} %refs_2_.25, bf16[64,4096]{1,0:T(8,128)(2,1)} %refs_2_.18, f32[1,512]{1,0:T(1,128)} %bitcast.14, ...), custom_call_target="tpu_custom_call" | custom-call | flops 9646899200 | tf_op jit(solution)/shard_map/prior_first/pallas_call | solution.py:139
  12.8 2.6 %collective-permute-start.3 = (f32[16,1024]{1,0:T(8,128)}, f32[16,1024]{1,0:T(8,128)S(1)}, u32[]{:S(2)}, u32[]{:S(2)}) collective-permute-start(f32[16,1024]{1,0:T(8,128)} %bitcast.12), channel_id=1, source_target_pairs={{0,1},{1,0},{2,3},{3,2},{4,5},{5,4},{6,7},{7,6},{8,9},{9,8},{10,11... | collective-permute-start | bytes 196616 | tf_op jit(solution)/shard_map/ppermute | solution.py:494
  16.6 8.9 %prior_mine.1.refs_0_.refs_2_.refs_5_ = f32[64,1024]{1,0:T(8,128)S(1)} custom-call(s32[2,64]{1,0:T(2,128)S(1)} %copy-done.1, bf16[2048,128]{1,0:T(8,128)(2,1)S(1)} %copy-done.7, bf16[64,4096]{1,0:T(8,128)(2,1)S(1)} %copy-done.2, f32[8,4096]{1,0:T(8,128)S(1)} %copy-done.5, f32[1,512]{1,0:T(1,128)S(1)} %bitcast.15, f32[64,512]{1,0:T(8,128)S(1)} %copy-done.4), custom_call_target="tpu_custom_call" | custom-call | flops 9646899200 | tf_op jit(solution)/shard_map/prior_mine/pallas_call | solution.py:139
  25.6 2.5 %collective-permute-start.4 = (f32[16,1024]{1,0:T(8,128)S(1)}, f32[16,1024]{1,0:T(8,128)S(1)}, u32[]{:S(2)}, u32[]{:S(2)}) collective-permute-start(f32[16,1024]{1,0:T(8,128)S(1)} %rows_0.1.refs_0_), channel_id=1, source_target_pairs={{0,3},{1,2},{2,1},{3,0},{4,7},{5,6},{6,5},{7,4},{8,11},{9,10},{10,... | collective-permute-start | bytes 196616 | tf_op jit(solution)/shard_map/ppermute | solution.py:494
  28.2 1.6 %collective-permute-start.1 = (f32[32,1024]{1,0:T(8,128)S(1)}, f32[32,1024]{1,0:T(8,128)S(1)}, u32[]{:S(2)}, u32[]{:S(2)}) collective-permute-start(f32[32,1024]{1,0:T(8,128)S(1)} %get-tuple-element.35.refs_6_.refs_0_), channel_id=1, source_target_pairs={{0,8},{4,12},{8,0},{12,4},{16,24},{20,28},{24,16},{28,20},{1,9},{5... | collective-permute-start | bytes 393224 | tf_op jit(solution)/shard_map/ppermute | solution.py:494
  29.7 1.5 %collective-permute-start.2 = (f32[32,1024]{1,0:T(8,128)S(1)}, f32[32,1024]{1,0:T(8,128)S(1)}, u32[]{:S(2)}, u32[]{:S(2)}) collective-permute-start(f32[32,1024]{1,0:T(8,128)S(1)} %get-tuple-element.36.refs_1_), channel_id=1, source_target_pairs={{0,16},{4,20},{8,24},{12,28},{16,0},{20,4},{24,8},{28,12},{1,17},{... | collective-permute-start | bytes 393224 | tf_op jit(solution)/shard_map/ppermute | solution.py:494
  31.3 4.7 %prior_0_0.1.refs_2_.refs_4_ = f32[64,512]{1,0:T(8,128)S(1)} custom-call(s32[2,64]{1,0:T(2,128)S(1)} %copy-done.1, bf16[2048,128]{1,0:T(8,128)(2,1)S(1)} %copy-done.8, bf16[64,4096]{1,0:T(8,128)(2,1)S(1)} %copy-done.2, f32[8,4096]{1,0:T(8,128)S(1)} %copy-done.5, f32[1,512]{1,0:T(1,128)S(1)} %bitcast.16, f32[64,512]{1,0:T(8,128)S(1)} %copy-done.4, ...), custom_call_target="tpu_custom_call" | custom-call | flops 4823449600 | tf_op jit(solution)/shard_map/prior_0_0/pallas_call | solution.py:139
  37.2 4.9 %prior_0_4.1.refs_2_.refs_4_ = f32[64,512]{1,0:T(8,128)S(1)} custom-call(s32[2,64]{1,0:T(2,128)S(1)} %copy-done.1, bf16[2048,128]{1,0:T(8,128)(2,1)S(1)} %copy-done.8, bf16[64,4096]{1,0:T(8,128)(2,1)S(1)} %copy-done.2, f32[8,4096]{1,0:T(8,128)S(1)} %copy-done.5, f32[1,512]{1,0:T(1,128)S(1)} %bitcast.17, f32[64,512]{1,0:T(8,128)S(1)} %copy-done.4, ...), custom_call_target="tpu_custom_call" | custom-call | flops 4823449600 | tf_op jit(solution)/shard_map/prior_0_4/pallas_call | solution.py:139
  42.7 1.5 %inverse_0_mine.1.refs_2_ = f32[64,1024]{1,0:T(8,128)S(1)} custom-call(f32[64,1024]{1,0:T(8,128)S(1)} %wide_0_1.1.refs_0_, f32[2,1024,2048]{2,1,0:T(8,128)S(1)} %bitcast.8), custom_call_target="tpu_custom_call" | custom-call | flops 536870912 | tf_op jit(solution)/shard_map/inverse_0_mine/pallas_call | solution.py:139
  44.2 1.5 %inverse_0_theirs.1 = f32[64,1024]{1,0:T(8,128)S(1)} custom-call(f32[64,1024]{1,0:T(8,128)S(1)} %collective-permute-done.7.refs_0_, f32[2,1024,2048]{2,1,0:T(8,128)S(1)} %bitcast.8, f32[64,1024]{1,0:T(8,128)S(1)} %inverse_0_mine.1.refs_2_), custom_call_target="tpu_custom_call" | custom-call | flops 536870912 | tf_op jit(solution)/shard_map/inverse_0_theirs/pallas_call | solution.py:139
  47.3 3.0 %tiles_0_0.1 = (bf16[1024,1024]{1,0:T(8,128)(2,1)S(1)}, bf16[1024,1024]{1,0:T(8,128)(2,1)S(1)}) custom-call(s32[2,64]{1,0:T(2,128)S(1)} %copy-done.1, bf16[2,1024,64]{2,1,0:T(8,128)(2,1)S(1)} %lefts.1.refs_5_.refs_1_, f32[8,4096]{1,0:T(8,128)S(1)} %copy-done.5, f32[8,1]{1,0:T(8,128)S(1)} %copy.11.refs_1_.refs_3_, ...), custom_call_target="tpu_custom_call" | custom-call | flops 314572800 | tf_op jit(solution)/shard_map/tiles_0_0/pallas_call | solution.py:139
  50.3 4.7 %prior_1_0.1.refs_4_ = f32[64,512]{1,0:T(8,128)S(1)} custom-call(s32[2,64]{1,0:T(2,128)S(1)} %copy-done.1, bf16[2048,128]{1,0:T(8,128)(2,1)S(1)} %copy-done.8, bf16[64,4096]{1,0:T(8,128)(2,1)S(1)} %copy-done.2, f32[8,4096]{1,0:T(8,128)S(1)} %copy-done.5, f32[1,512]{1,0:T(1,128)S(1)} %bitcast.18, f32[64,512]{1,0:T(8,128)S(1)} %copy-done.4, ...), custom_call_target="tpu_custom_call" | custom-call | flops 838860800 | tf_op jit(solution)/shard_map/prior_1_0/pallas_call | solution.py:139
  55.1 3.0 %collective-permute-start.10 = (f32[32,1024]{1,0:T(8,128)S(1)}, f32[32,1024]{1,0:T(8,128)S(1)}, u32[]{:S(2)}, u32[]{:S(2)}) collective-permute-start(f32[32,1024]{1,0:T(8,128)S(1)} %get-tuple-element.42.refs_6_.refs_4_.refs_0_), channel_id=1, source_target_pairs={{0,3},{1,2},{2,1},{3,0},{4,7},{5,6},{6,5},{7,4},{8,11},{9,10},{10,... | collective-permute-start | bytes 393224 | tf_op jit(solution)/shard_map/ppermute | solution.py:494
  58.1 3.0 %tiles_0_1.1 = (bf16[1024,1024]{1,0:T(8,128)(2,1)S(1)}, bf16[1024,1024]{1,0:T(8,128)(2,1)S(1)}) custom-call(s32[2,64]{1,0:T(2,128)S(1)} %copy-done.1, bf16[2,1024,64]{2,1,0:T(8,128)(2,1)S(1)} %lefts.1.refs_5_.refs_1_, f32[8,4096]{1,0:T(8,128)S(1)} %copy-done.5, f32[8,1]{1,0:T(8,128)S(1)} %copy.11.refs_1_.refs_3_, ...), custom_call_target="tpu_custom_call" | custom-call | flops 314572800 | tf_op jit(solution)/shard_map/tiles_0_1/pallas_call | solution.py:139
  61.2 5.0 %prior_1_4.1.refs_4_ = f32[64,512]{1,0:T(8,128)S(1)} custom-call(s32[2,64]{1,0:T(2,128)S(1)} %copy-done.1, bf16[2048,128]{1,0:T(8,128)(2,1)S(1)} %copy-done.8, bf16[64,4096]{1,0:T(8,128)(2,1)S(1)} %copy-done.2, f32[8,4096]{1,0:T(8,128)S(1)} %copy-done.5, f32[1,512]{1,0:T(1,128)S(1)} %bitcast.19, f32[64,512]{1,0:T(8,128)S(1)} %copy-done.4, ...), custom_call_target="tpu_custom_call" | custom-call | flops 838860800 | tf_op jit(solution)/shard_map/prior_1_4/pallas_call | solution.py:139
  68.6 1.6 %collective-permute-start.13 = (f32[32,1024]{1,0:T(8,128)S(1)}, f32[32,1024]{1,0:T(8,128)S(1)}, u32[]{:S(2)}, u32[]{:S(2)}) collective-permute-start(f32[32,1024]{1,0:T(8,128)S(1)} %get-tuple-element.46.refs_6_.refs_0_), channel_id=1, source_target_pairs={{0,8},{4,12},{8,0},{12,4},{16,24},{20,28},{24,16},{28,20},{1,9},{5... | collective-permute-start | bytes 393224 | tf_op jit(solution)/shard_map/ppermute | solution.py:494
  70.2 1.5 %collective-permute-start.14 = (f32[32,1024]{1,0:T(8,128)S(1)}, f32[32,1024]{1,0:T(8,128)S(1)}, u32[]{:S(2)}, u32[]{:S(2)}) collective-permute-start(f32[32,1024]{1,0:T(8,128)S(1)} %get-tuple-element.47.refs_1_), channel_id=1, source_target_pairs={{0,16},{4,20},{8,24},{12,28},{16,0},{20,4},{24,8},{28,12},{1,17},{... | collective-permute-start | bytes 393224 | tf_op jit(solution)/shard_map/ppermute | solution.py:494
  71.7 3.6 %fused_0.1.refs_4_.refs_3_ = f32[64,1024]{1,0:T(8,128)S(1)} custom-call(s32[2,64]{1,0:T(2,128)S(1)} %copy-done.1, bf16[2,1024,64]{2,1,0:T(8,128)(2,1)S(1)} %lefts.1.refs_5_.refs_1_, f32[8,4096]{1,0:T(8,128)S(1)} %copy-done.5, f32[8,1]{1,0:T(8,128)S(1)} %copy.11.refs_1_.refs_3_, f32[64,1024]{1,0:T(8,128)S(1)} %narrow_0_1.1.refs_0_.refs_4_.refs_2_, ...), custom_call_target="tpu_custom_call" | custom-call | flops 1677721600 | tf_op jit(solution)/shard_map/fused_0/pallas_call | solution.py:139
  75.5 1.6 %collective-permute-start.15 = (f32[32,1024]{1,0:T(8,128)S(1)}, f32[32,1024]{1,0:T(8,128)S(1)}, u32[]{:S(2)}, u32[]{:S(2)}) collective-permute-start(f32[32,1024]{1,0:T(8,128)S(1)} %get-tuple-element.48.refs_6_.refs_0_), channel_id=1, source_target_pairs={{0,16},{4,20},{8,24},{12,28},{16,0},{20,4},{24,8},{28,12},{1,17},{... | collective-permute-start | bytes 393224 | tf_op jit(solution)/shard_map/ppermute | solution.py:494
  77.7 3.6 %fused_1.1.refs_4_ = f32[64,1024]{1,0:T(8,128)S(1)} custom-call(s32[2,64]{1,0:T(2,128)S(1)} %copy-done.1, bf16[2,1024,64]{2,1,0:T(8,128)(2,1)S(1)} %lefts.1.refs_5_.refs_1_, f32[8,4096]{1,0:T(8,128)S(1)} %copy-done.5, f32[8,1]{1,0:T(8,128)S(1)} %copy.11.refs_1_.refs_3_, f32[64,1024]{1,0:T(8,128)S(1)} %narrow_0_1.1.refs_0_.refs_4_.refs_2_, ...), custom_call_target="tpu_custom_call" | custom-call | flops 1677721600 | tf_op jit(solution)/shard_map/fused_1/pallas_call | solution.py:139
  82.2 1.5 %inverse_1_mine.1.refs_2_ = f32[64,1024]{1,0:T(8,128)S(1)} custom-call(f32[64,1024]{1,0:T(8,128)S(1)} %wide_1_1.1.refs_0_, f32[2,1024,2048]{2,1,0:T(8,128)S(1)} %bitcast.8), custom_call_target="tpu_custom_call" | custom-call | flops 536870912 | tf_op jit(solution)/shard_map/inverse_1_mine/pallas_call | solution.py:139
  85.2 2.1 %collective-permute-start.18 = (f32[32,1024]{1,0:T(8,128)S(1)}, f32[32,1024]{1,0:T(8,128)S(1)}, u32[]{:S(2)}, u32[]{:S(2)}) collective-permute-start(f32[32,1024]{1,0:T(8,128)S(1)} %get-tuple-element.65.refs_4_.refs_0_), channel_id=1, source_target_pairs={{0,1},{1,0},{2,3},{3,2},{4,5},{5,4},{6,7},{7,6},{8,9},{9,8},{10,11... | collective-permute-start | bytes 393224 | tf_op jit(solution)/shard_map/ppermute | solution.py:494
  88.2 3.0 %tiles_1_0_2.1 = (bf16[1024,1024]{1,0:T(8,128)(2,1)S(1)}, bf16[1024,1024]{1,0:T(8,128)(2,1)S(1)}) custom-call(s32[2,64]{1,0:T(2,128)S(1)} %copy-done.1, bf16[2,1024,64]{2,1,0:T(8,128)(2,1)S(1)} %lefts.1.refs_5_.refs_1_, f32[8,4096]{1,0:T(8,128)S(1)} %copy-done.5, f32[8,1]{1,0:T(8,128)S(1)} %copy.11.refs_1_.refs_3_, ...), custom_call_target="tpu_custom_call" | custom-call | flops 314572800 | tf_op jit(solution)/shard_map/tiles_1_0_2/pallas_call | solution.py:139
  91.2 3.0 %tiles_1_0_0.1 = (bf16[1024,1024]{1,0:T(8,128)(2,1)S(1)}, bf16[1024,1024]{1,0:T(8,128)(2,1)S(1)}) custom-call(s32[2,64]{1,0:T(2,128)S(1)} %copy-done.1, bf16[2,1024,64]{2,1,0:T(8,128)(2,1)S(1)} %lefts.1.refs_5_.refs_1_, f32[8,4096]{1,0:T(8,128)S(1)} %copy-done.5, f32[8,1]{1,0:T(8,128)S(1)} %copy.11.refs_1_.refs_3_, ...), custom_call_target="tpu_custom_call" | custom-call | flops 314572800 | tf_op jit(solution)/shard_map/tiles_1_0_0/pallas_call | solution.py:139
  95.0 2.9 %collective-permute-start.20 = (f32[32,1024]{1,0:T(8,128)S(1)}, f32[32,1024]{1,0:T(8,128)S(1)}, u32[]{:S(2)}, u32[]{:S(2)}) collective-permute-start(f32[32,1024]{1,0:T(8,128)S(1)} %get-tuple-element.54.refs_4_.refs_7_.refs_0_), channel_id=1, source_target_pairs={{0,3},{1,2},{2,1},{3,0},{4,7},{5,6},{6,5},{7,4},{8,11},{9,10},{10,... | collective-permute-start | bytes 393224 | tf_op jit(solution)/shard_map/ppermute | solution.py:494
  99.2 3.0 %tiles_1_1_2.1 = (bf16[1024,1024]{1,0:T(8,128)(2,1)S(1)}, bf16[1024,1024]{1,0:T(8,128)(2,1)S(1)}) custom-call(s32[2,64]{1,0:T(2,128)S(1)} %copy-done.1, bf16[2,1024,64]{2,1,0:T(8,128)(2,1)S(1)} %lefts.1.refs_5_.refs_1_, f32[8,4096]{1,0:T(8,128)S(1)} %copy-done.5, f32[8,1]{1,0:T(8,128)S(1)} %copy.11.refs_1_.refs_3_, ...), custom_call_target="tpu_custom_call" | custom-call | flops 314572800 | tf_op jit(solution)/shard_map/tiles_1_1_2/pallas_call | solution.py:139
  102.2 3.0 %tiles_1_1_0.1 = (bf16[1024,1024]{1,0:T(8,128)(2,1)S(1)}, bf16[1024,1024]{1,0:T(8,128)(2,1)S(1)}) custom-call(s32[2,64]{1,0:T(2,128)S(1)} %copy-done.1, bf16[2,1024,64]{2,1,0:T(8,128)(2,1)S(1)} %lefts.1.refs_5_.refs_1_, f32[8,4096]{1,0:T(8,128)S(1)} %copy-done.5, f32[8,1]{1,0:T(8,128)S(1)} %copy.11.refs_1_.refs_3_, ...), custom_call_target="tpu_custom_call" | custom-call | flops 314572800 | tf_op jit(solution)/shard_map/tiles_1_1_0/pallas_call | solution.py:139
  105.3 2.2 %last_0.1 = f32[4,64,512]{2,1,0:T(8,128)S(1)} custom-call(s32[2,64]{1,0:T(2,128)S(1)} %copy-done.1, f32[64,1024]{1,0:T(8,128)S(1)} %narrow_1_1.1.refs_1_, f32[8,64,512]{2,1,0:T(8,128)S(1)} %arrange.1.refs_8_.refs_2_, bf16[1024,1024]{1,0:T(8,128)(2,1)S(1)} %get-tuple-element.50.refs_4_.refs_3_, bf16[1024,1024]{1,0:T(8,128)(2,1)S(1)} %get-tuple-element.51.refs_5_.refs_4_, ...), custom_call_target="tpu_custom_call" | custom-call | flops 805306368 | tf_op jit(solution)/shard_map/last_0/pallas_call | solution.py:139
  107.6 2.2 %last_1.1.refs_0_ = f32[4,64,512]{2,1,0:T(8,128)S(1)} custom-call(s32[2,64]{1,0:T(2,128)S(1)} %copy-done.1, f32[64,1024]{1,0:T(8,128)S(1)} %narrow_1_1.1.refs_1_, f32[8,64,512]{2,1,0:T(8,128)S(1)} %arrange.1.refs_8_.refs_2_, bf16[1024,1024]{1,0:T(8,128)(2,1)S(1)} %get-tuple-element.56.refs_4_.refs_3_, ...), custom_call_target="tpu_custom_call" | custom-call | flops 805306368 | tf_op jit(solution)/shard_map/last_1/pallas_call | solution.py:139
  111.1 2.5 %collective-permute-start.25 = (f32[64,512]{1,0:T(8,128)S(1)}, f32[64,512]{1,0:T(8,128)S(1)}, u32[]{:S(2)}, u32[]{:S(2)}) collective-permute-start(f32[64,512]{1,0:T(8,128)S(1)} %get-tuple-element.63), channel_id=1, source_target_pairs={{0,24},{4,28},{8,16},{12,20},{16,8},{20,12},{24,0},{28,4},{1,25},{... | collective-permute-start | bytes 393224 | tf_op jit(solution)/shard_map/ppermute | solution.py:494
  114.4 2.0 %collective-permute-done.23 = f32[64,512]{1,0:T(8,128)S(1)} collective-permute-done((f32[64,512]{1,0:T(8,128)S(1)}, f32[64,512]{1,0:T(8,128)S(1)}, u32[]{:S(2)}, u32[]{:S(2)}) %collective-permute-start.23) | collective-permute-done | bytes 131104 | tf_op jit(solution)/shard_map/ppermute | solution.py:494
  116.4 2.6 %collective-permute-done.24 = f32[64,512]{1,0:T(8,128)S(1)} collective-permute-done((f32[64,512]{1,0:T(8,128)S(1)}, f32[64,512]{1,0:T(8,128)S(1)}, u32[]{:S(2)}, u32[]{:S(2)}) %collective-permute-start.24) | collective-permute-done | bytes 131104 | tf_op jit(solution)/shard_map/ppermute | solution.py:494
  (93 shorter events, 16.5 us)
Async XLA Ops:
  0.6 14.9 %copy-start.1 = (s32[2,64]{1,0:T(2,128)S(1)}, s32[2,64]{1,0:T(2,128)}, u32[]{:S(2)}) copy-start(s32[2,64]{1,0:T(2,128)} %refs_0_.33) | copy-start | bytes 1540
  0.6 14.8 %copy-start.2 = (bf16[64,4096]{1,0:T(8,128)(2,1)S(1)}, bf16[64,4096]{1,0:T(8,128)(2,1)}, u32[]{:S(2)}) copy-start(bf16[64,4096]{1,0:T(8,128)(2,1)} %refs_2_.18) | copy-start | bytes 1572868
  0.7 14.8 %copy-start.4 = (f32[64,512]{1,0:T(8,128)S(1)}, f32[64,512]{1,0:T(8,128)}, u32[]{:S(2)}) copy-start(f32[64,512]{1,0:T(8,128)} %refs_5_.9) | copy-start | bytes 393220
  0.7 14.8 %copy-start.5 = (f32[8,4096]{1,0:T(8,128)S(1)}, f32[8,4096]{1,0:T(8,128)}, u32[]{:S(2)}) copy-start(f32[8,4096]{1,0:T(8,128)} %refs_2_.25) | copy-start | bytes 393220
  0.7 14.8 %copy-start.6 = (f32[512]{0:T(512)S(1)}, f32[512]{0:T(512)}, u32[]{:S(2)}) copy-start(f32[512]{0:T(512)} %param.14) | copy-start | bytes 6148
  12.3 15.8 %collective-permute-start = (f32[64,1024]{1,0:T(8,128)}, f32[64,1024]{1,0:T(8,128)S(1)}, u32[]{:S(2)}, u32[]{:S(2)}) collective-permute-start(f32[64,1024]{1,0:T(8,128)} %get-tuple-element.34.refs_5_), channel_id=1, source_target_pairs={{0,4},{4,0},{8,12},{12,8},{16,20},{20,16},{24,28},{28,24},{1,5},{5... | collective-permute-start | bytes 786440 | tf_op jit(solution)/shard_map/ppermute | solution.py:494
  12.8 12.7 %collective-permute-start.3 = (f32[16,1024]{1,0:T(8,128)}, f32[16,1024]{1,0:T(8,128)S(1)}, u32[]{:S(2)}, u32[]{:S(2)}) collective-permute-start(f32[16,1024]{1,0:T(8,128)} %bitcast.12), channel_id=1, source_target_pairs={{0,1},{1,0},{2,3},{3,2},{4,5},{5,4},{6,7},{7,6},{8,9},{9,8},{10,11... | collective-permute-start | bytes 196616 | tf_op jit(solution)/shard_map/ppermute | solution.py:494
  16.6 14.7 %copy-start.8 = (bf16[2048,128]{1,0:T(8,128)(2,1)S(1)}, bf16[2048,128]{1,0:T(8,128)(2,1)}, u32[]{:S(2)}) copy-start(bf16[2048,128]{1,0:T(8,128)(2,1)} %get-tuple-element.33.refs_1_) | copy-start | bytes 1572868
  25.6 10.4 %collective-permute-start.4 = (f32[16,1024]{1,0:T(8,128)S(1)}, f32[16,1024]{1,0:T(8,128)S(1)}, u32[]{:S(2)}, u32[]{:S(2)}) collective-permute-start(f32[16,1024]{1,0:T(8,128)S(1)} %rows_0.1.refs_0_), channel_id=1, source_target_pairs={{0,3},{1,2},{2,1},{3,0},{4,7},{5,6},{6,5},{7,4},{8,11},{9,10},{10,... | collective-permute-start | bytes 196616 | tf_op jit(solution)/shard_map/ppermute | solution.py:494
  28.2 7.9 %collective-permute-start.1 = (f32[32,1024]{1,0:T(8,128)S(1)}, f32[32,1024]{1,0:T(8,128)S(1)}, u32[]{:S(2)}, u32[]{:S(2)}) collective-permute-start(f32[32,1024]{1,0:T(8,128)S(1)} %get-tuple-element.35.refs_6_.refs_0_), channel_id=1, source_target_pairs={{0,8},{4,12},{8,0},{12,4},{16,24},{20,28},{24,16},{28,20},{1,9},{5... | collective-permute-start | bytes 393224 | tf_op jit(solution)/shard_map/ppermute | solution.py:494
  29.7 6.3 %collective-permute-start.2 = (f32[32,1024]{1,0:T(8,128)S(1)}, f32[32,1024]{1,0:T(8,128)S(1)}, u32[]{:S(2)}, u32[]{:S(2)}) collective-permute-start(f32[32,1024]{1,0:T(8,128)S(1)} %get-tuple-element.36.refs_1_), channel_id=1, source_target_pairs={{0,16},{4,20},{8,24},{12,28},{16,0},{20,4},{24,8},{28,12},{1,17},{... | collective-permute-start | bytes 393224 | tf_op jit(solution)/shard_map/ppermute | solution.py:494
  36.1 6.4 %collective-permute-start.5 = (f32[32,1024]{1,0:T(8,128)S(1)}, f32[32,1024]{1,0:T(8,128)S(1)}, u32[]{:S(2)}, u32[]{:S(2)}) collective-permute-start(f32[32,1024]{1,0:T(8,128)S(1)} %get-tuple-element.38.refs_6_.refs_0_), channel_id=1, source_target_pairs={{0,16},{4,20},{8,24},{12,28},{16,0},{20,4},{24,8},{28,12},{1,17},{... | collective-permute-start | bytes 393224 | tf_op jit(solution)/shard_map/ppermute | solution.py:494
  36.7 5.9 %collective-permute-start.6 = (f32[32,1024]{1,0:T(8,128)S(1)}, f32[32,1024]{1,0:T(8,128)S(1)}, u32[]{:S(2)}, u32[]{:S(2)}) collective-permute-start(f32[32,1024]{1,0:T(8,128)S(1)} %get-tuple-element.39.refs_1_), channel_id=1, source_target_pairs={{0,8},{4,12},{8,0},{12,4},{16,24},{20,28},{24,16},{28,20},{1,9},{5... | collective-permute-start | bytes 393224 | tf_op jit(solution)/shard_map/ppermute | solution.py:494
  42.6 1.6 %collective-permute-start.7 = (f32[64,1024]{1,0:T(8,128)S(1)}, f32[64,1024]{1,0:T(8,128)S(1)}, u32[]{:S(2)}, u32[]{:S(2)}) collective-permute-start(f32[64,1024]{1,0:T(8,128)S(1)} %wide_0_1.1.refs_0_), channel_id=1, source_target_pairs={{0,4},{4,0},{8,12},{12,8},{16,20},{20,16},{24,28},{28,24},{1,5},{5... | collective-permute-start | bytes 786440 | tf_op jit(solution)/shard_map/ppermute | solution.py:494
  45.7 9.4 %collective-permute-start.8 = (f32[32,1024]{1,0:T(8,128)S(1)}, f32[32,1024]{1,0:T(8,128)S(1)}, u32[]{:S(2)}, u32[]{:S(2)}) collective-permute-start(f32[32,1024]{1,0:T(8,128)S(1)} %get-tuple-element.67.refs_6_.refs_4_.refs_0_), channel_id=1, source_target_pairs={{0,1},{1,0},{2,3},{3,2},{4,5},{5,4},{6,7},{7,6},{8,9},{9,8},{10,11... | collective-permute-start | bytes 393224 | tf_op jit(solution)/shard_map/ppermute | solution.py:494
  46.4 8.7 %collective-permute-start.9 = (f32[32,1024]{1,0:T(8,128)S(1)}, f32[32,1024]{1,0:T(8,128)S(1)}, u32[]{:S(2)}, u32[]{:S(2)}) collective-permute-start(f32[32,1024]{1,0:T(8,128)S(1)} %get-tuple-element.66.refs_1_), channel_id=1, source_target_pairs={{0,3},{1,2},{2,1},{3,0},{4,7},{5,6},{6,5},{7,4},{8,11},{9,10},{10,... | collective-permute-start | bytes 393224 | tf_op jit(solution)/shard_map/ppermute | solution.py:494
  55.1 11.0 %collective-permute-start.10 = (f32[32,1024]{1,0:T(8,128)S(1)}, f32[32,1024]{1,0:T(8,128)S(1)}, u32[]{:S(2)}, u32[]{:S(2)}) collective-permute-start(f32[32,1024]{1,0:T(8,128)S(1)} %get-tuple-element.42.refs_6_.refs_4_.refs_0_), channel_id=1, source_target_pairs={{0,3},{1,2},{2,1},{3,0},{4,7},{5,6},{6,5},{7,4},{8,11},{9,10},{10,... | collective-permute-start | bytes 393224 | tf_op jit(solution)/shard_map/ppermute | solution.py:494
  58.1 8.0 %collective-permute-start.11 = (f32[32,1024]{1,0:T(8,128)S(1)}, f32[32,1024]{1,0:T(8,128)S(1)}, u32[]{:S(2)}, u32[]{:S(2)}) collective-permute-start(f32[32,1024]{1,0:T(8,128)S(1)} %get-tuple-element.43.refs_1_), channel_id=1, source_target_pairs={{0,1},{1,0},{2,3},{3,2},{4,5},{5,4},{6,7},{7,6},{8,9},{9,8},{10,11... | collective-permute-start | bytes 393224 | tf_op jit(solution)/shard_map/ppermute | solution.py:494
  67.0 1.6 %collective-permute-start.12 = (f32[64,1024]{1,0:T(8,128)S(1)}, f32[64,1024]{1,0:T(8,128)S(1)}, u32[]{:S(2)}, u32[]{:S(2)}) collective-permute-start(f32[64,1024]{1,0:T(8,128)S(1)} %product_0_0.1.refs_5_), channel_id=1, source_target_pairs={{0,4},{4,0},{8,12},{12,8},{16,20},{20,16},{24,28},{28,24},{1,5},{5... | collective-permute-start | bytes 786440 | tf_op jit(solution)/shard_map/ppermute | solution.py:494
  68.6 6.7 %collective-permute-start.13 = (f32[32,1024]{1,0:T(8,128)S(1)}, f32[32,1024]{1,0:T(8,128)S(1)}, u32[]{:S(2)}, u32[]{:S(2)}) collective-permute-start(f32[32,1024]{1,0:T(8,128)S(1)} %get-tuple-element.46.refs_6_.refs_0_), channel_id=1, source_target_pairs={{0,8},{4,12},{8,0},{12,4},{16,24},{20,28},{24,16},{28,20},{1,9},{5... | collective-permute-start | bytes 393224 | tf_op jit(solution)/shard_map/ppermute | solution.py:494
  70.2 5.3 %collective-permute-start.14 = (f32[32,1024]{1,0:T(8,128)S(1)}, f32[32,1024]{1,0:T(8,128)S(1)}, u32[]{:S(2)}, u32[]{:S(2)}) collective-permute-start(f32[32,1024]{1,0:T(8,128)S(1)} %get-tuple-element.47.refs_1_), channel_id=1, source_target_pairs={{0,16},{4,20},{8,24},{12,28},{16,0},{20,4},{24,8},{28,12},{1,17},{... | collective-permute-start | bytes 393224 | tf_op jit(solution)/shard_map/ppermute | solution.py:494
  75.5 5.7 %collective-permute-start.15 = (f32[32,1024]{1,0:T(8,128)S(1)}, f32[32,1024]{1,0:T(8,128)S(1)}, u32[]{:S(2)}, u32[]{:S(2)}) collective-permute-start(f32[32,1024]{1,0:T(8,128)S(1)} %get-tuple-element.48.refs_6_.refs_0_), channel_id=1, source_target_pairs={{0,16},{4,20},{8,24},{12,28},{16,0},{20,4},{24,8},{28,12},{1,17},{... | collective-permute-start | bytes 393224 | tf_op jit(solution)/shard_map/ppermute | solution.py:494
  77.1 5.0 %collective-permute-start.16 = (f32[32,1024]{1,0:T(8,128)S(1)}, f32[32,1024]{1,0:T(8,128)S(1)}, u32[]{:S(2)}, u32[]{:S(2)}) collective-permute-start(f32[32,1024]{1,0:T(8,128)S(1)} %get-tuple-element.49.refs_1_), channel_id=1, source_target_pairs={{0,8},{4,12},{8,0},{12,4},{16,24},{20,28},{24,16},{28,20},{1,9},{5... | collective-permute-start | bytes 393224 | tf_op jit(solution)/shard_map/ppermute | solution.py:494
  82.1 1.6 %collective-permute-start.17 = (f32[64,1024]{1,0:T(8,128)S(1)}, f32[64,1024]{1,0:T(8,128)S(1)}, u32[]{:S(2)}, u32[]{:S(2)}) collective-permute-start(f32[64,1024]{1,0:T(8,128)S(1)} %wide_1_1.1.refs_0_), channel_id=1, source_target_pairs={{0,4},{4,0},{8,12},{12,8},{16,20},{20,16},{24,28},{28,24},{1,5},{5... | collective-permute-start | bytes 786440 | tf_op jit(solution)/shard_map/ppermute | solution.py:494
  85.2 9.1 %collective-permute-start.18 = (f32[32,1024]{1,0:T(8,128)S(1)}, f32[32,1024]{1,0:T(8,128)S(1)}, u32[]{:S(2)}, u32[]{:S(2)}) collective-permute-start(f32[32,1024]{1,0:T(8,128)S(1)} %get-tuple-element.65.refs_4_.refs_0_), channel_id=1, source_target_pairs={{0,1},{1,0},{2,3},{3,2},{4,5},{5,4},{6,7},{7,6},{8,9},{9,8},{10,11... | collective-permute-start | bytes 393224 | tf_op jit(solution)/shard_map/ppermute | solution.py:494
  87.3 7.7 %collective-permute-start.19 = (f32[32,1024]{1,0:T(8,128)S(1)}, f32[32,1024]{1,0:T(8,128)S(1)}, u32[]{:S(2)}, u32[]{:S(2)}) collective-permute-start(f32[32,1024]{1,0:T(8,128)S(1)} %get-tuple-element.64.refs_1_), channel_id=1, source_target_pairs={{0,3},{1,2},{2,1},{3,0},{4,7},{5,6},{6,5},{7,4},{8,11},{9,10},{10,... | collective-permute-start | bytes 393224 | tf_op jit(solution)/shard_map/ppermute | solution.py:494
  95.0 10.3 %collective-permute-start.20 = (f32[32,1024]{1,0:T(8,128)S(1)}, f32[32,1024]{1,0:T(8,128)S(1)}, u32[]{:S(2)}, u32[]{:S(2)}) collective-permute-start(f32[32,1024]{1,0:T(8,128)S(1)} %get-tuple-element.54.refs_4_.refs_7_.refs_0_), channel_id=1, source_target_pairs={{0,3},{1,2},{2,1},{3,0},{4,7},{5,6},{6,5},{7,4},{8,11},{9,10},{10,... | collective-permute-start | bytes 393224 | tf_op jit(solution)/shard_map/ppermute | solution.py:494
  97.8 7.4 %collective-permute-start.21 = (f32[32,1024]{1,0:T(8,128)S(1)}, f32[32,1024]{1,0:T(8,128)S(1)}, u32[]{:S(2)}, u32[]{:S(2)}) collective-permute-start(f32[32,1024]{1,0:T(8,128)S(1)} %get-tuple-element.55.refs_1_), channel_id=1, source_target_pairs={{0,1},{1,0},{2,3},{3,2},{4,5},{5,4},{6,7},{7,6},{8,9},{9,8},{10,11... | collective-permute-start | bytes 393224 | tf_op jit(solution)/shard_map/ppermute | solution.py:494
  107.6 2.3 %collective-permute-start.22 = (f32[4,64,512]{2,1,0:T(8,128)S(1)}, f32[4,64,512]{2,1,0:T(8,128)S(1)}, u32[]{:S(2)}, u32[]{:S(2)}) collective-permute-start(f32[4,64,512]{2,1,0:T(8,128)S(1)} %last_0.1), channel_id=1, source_target_pairs={{0,4},{4,0},{8,12},{12,8},{16,20},{20,16},{24,28},{28,24},{1,5},{5... | collective-permute-start | bytes 1572872 | tf_op jit(solution)/shard_map/ppermute | solution.py:494
  110.0 6.4 %collective-permute-start.23 = (f32[64,512]{1,0:T(8,128)S(1)}, f32[64,512]{1,0:T(8,128)S(1)}, u32[]{:S(2)}, u32[]{:S(2)}) collective-permute-start(f32[64,512]{1,0:T(8,128)S(1)} %get-tuple-element.61), channel_id=1, source_target_pairs={{0,8},{4,12},{8,0},{12,4},{16,24},{20,28},{24,16},{28,20},{1,9},{5... | collective-permute-start | bytes 393224 | tf_op jit(solution)/shard_map/ppermute | solution.py:494
  110.6 8.4 %collective-permute-start.24 = (f32[64,512]{1,0:T(8,128)S(1)}, f32[64,512]{1,0:T(8,128)S(1)}, u32[]{:S(2)}, u32[]{:S(2)}) collective-permute-start(f32[64,512]{1,0:T(8,128)S(1)} %get-tuple-element.62), channel_id=1, source_target_pairs={{0,16},{4,20},{8,24},{12,28},{16,0},{20,4},{24,8},{28,12},{1,17},{... | collective-permute-start | bytes 393224 | tf_op jit(solution)/shard_map/ppermute | solution.py:494
  111.1 7.9 %collective-permute-start.25 = (f32[64,512]{1,0:T(8,128)S(1)}, f32[64,512]{1,0:T(8,128)S(1)}, u32[]{:S(2)}, u32[]{:S(2)}) collective-permute-start(f32[64,512]{1,0:T(8,128)S(1)} %get-tuple-element.63), channel_id=1, source_target_pairs={{0,24},{4,28},{8,16},{12,20},{16,8},{20,12},{24,0},{28,4},{1,25},{... | collective-permute-start | bytes 393224 | tf_op jit(solution)/shard_map/ppermute | solution.py:494
  (8 other events, 58.6 us)
